TPU v7x, 256 devices: a whole 4x4x8 slice. The times are simulated.
256 devices in a mesh: gx: 32 (over z, y), gy: 8 (over x, core).
Axes of the slice: x: 4, y: 4, z: 8, core: 2. Of those that a mesh axis runs over, the one named last changes fastest.
Arguments:
- cells: int32 [3, 524288], P(None, ('gx', 'gy')), may hold values from 0 to 511, as said below
- offsets: float32 [3, 524288], P(None, ('gx', 'gy')), may hold values from 0 to 1
- charges: float32 [524288], P(('gx', 'gy')), may hold values from -4 to 4
- kernel_weights: float32 [4, 3], replicated, may hold values from 0.25 to 1
- screening: float32 [1], replicated, may hold values from 0.1 to 0.4
Outputs:
- potential: float32 [524288], P(('gx', 'gy'))
- forces: float32 [3, 524288], P(None, ('gx', 'gy'))
Inputs may be any that keep to these rules, and one draw needn't show every extreme that they name: The particles of one device lie in that device's block of 16 x 32 x 512 fine cells and are sorted by cell; every device has a particle in the first and in the last cell of its block.
All inputs are finite; a program needn't handle non-finite values.
Results may differ from a plain program's by a relative error of at most 0.0003.
Values sent between devices are 32-bit elements; how exact they have to be, the bound alone decides.
A program may use at most 192 MiB of HBM per device.

v0:
```python
import math

import jax
import jax.numpy as jnp
import numpy as np
from jax import lax
from jax.experimental import pallas as pl
from jax.experimental.pallas import tpu as pltpu
from jax.sharding import PartitionSpec as P

CX, CY, NZ = 16, 32, 512
PART = 2048
CHUNK = 256
TERMS = 3
WIDTHS = (1.0, 1.5, 2.5)
TOP_WEIGHT = 0.0625
N_GX, N_GY = 32, 8
MESH = pl.DeviceIdType.MESH
F32, BF16 = jnp.float32, jnp.bfloat16

COUNT_X = (16, 8, 4, 2)
COUNT_Y = (32, 16, 8, 4)
GROUPS = (4, 2, 1, 1)
PITCH = (40, 24, 16, 16)
LANE_STEP = (1, 1, 1, 2)
NEAR_ONE = [math.exp(-1.0 / (s * s)) for s in WIDTHS]
NEAR_TWO = [math.exp(-4.0 / (s * s)) for s in WIDTHS]

FAR3 = [(dx, dy) for dx in (-2, -1, 0, 1, 2) for dy in (-1, 0, 1) if (dx, dy) != (0, 0)]

Y_OFFSET, C_OFFSET = {}, {}
for _l in range(3):
    for _t in range(3):
        for _g in range(GROUPS[_l]):
            Y_OFFSET[_l, _t, _g] = sum(
                3 * GROUPS[k] * (COUNT_X[k] + 1) for k in range(_l)
            ) + (_t * GROUPS[_l] + _g) * (COUNT_X[_l] + 1)
            C_OFFSET[_l, _t, _g] = 3 * len(C_OFFSET)
Y_ROWS = 280
C_ROWS = 64


def split(values):
    high = values.astype(BF16)
    return high, (values - high.astype(F32)).astype(BF16)


def dot3(left, right_high, right_low):
    high, low = split(left)
    return (
        jnp.dot(high, right_high, preferred_element_type=F32)
        + jnp.dot(low, right_high, preferred_element_type=F32)
        + jnp.dot(high, right_low, preferred_element_type=F32)
    )


def turn(values, shift):
    return pltpu.roll(values, shift % 128, 1)


def column_of(depth):
    return (depth & 3) * 128 + (depth >> 2)


def deposit_kernel(cells_s, cells_v, offsets_v, charges_v, out_ref):
    out_ref[...] = jnp.zeros_like(out_ref)
    pitch = PITCH[0]
    row = lax.broadcasted_iota(jnp.int32, (pitch, CHUNK), 0)
    depth_row = lax.broadcasted_iota(jnp.int32, (NZ, CHUNK), 0)
    for chunk in range(PART // CHUNK):
        part = pl.ds(chunk * CHUNK, CHUNK)
        x = cells_v[0:1, part] & (CX - 1)
        y = (cells_v[1:2, part] & (CY - 1)) + 2
        z = cells_v[2:3, part]
        fx, fy, fz = offsets_v[0:1, part], offsets_v[1:2, part], offsets_v[2:3, part]
        charge = charges_v[0:1, part]
        hot = jnp.where(depth_row == column_of(z), 1.0, 0.0).astype(BF16)
        across = jnp.where(row == y, 1.0 - fy, 0.0) + jnp.where(row == y + 1, fy, 0.0)
        first = cells_s[0, chunk * CHUNK] & (CX - 1)
        last = cells_s[0, chunk * CHUNK + CHUNK - 1] & (CX - 1)

        def plane(px, carry):
            here = jnp.where(x == px, charge, 0.0)
            low, high = here * (1.0 - fx), here * fx
            table = jnp.concatenate(
                [
                    across * (low * (1.0 - fz)),
                    across * (high * (1.0 - fz)),
                    across * (low * fz),
                    across * (high * fz),
                ],
                axis=0,
            )
            table_high, table_low = split(table)
            dims = (((1,), (1,)), ((), ()))
            spread = lax.dot_general(
                table_high, hot, dims, preferred_element_type=F32
            ) + lax.dot_general(table_low, hot, dims, preferred_element_type=F32)
            rows = pl.ds(pl.multiple_of(px * pitch, 8), 2 * pitch)
            for group in range(4):
                value = spread[: 2 * pitch, group * 128 : group * 128 + 128]
                if group:
                    above = spread[2 * pitch :, group * 128 - 128 : group * 128]
                else:
                    above = turn(spread[2 * pitch :, 384:512], 1)
                out_ref[group, rows, :] += value + above
            return carry

        lax.fori_loop(first, last + 1, plane, 0)


def sample_kernel(cells_s, cells_v, offsets_v, charges_v, field, potential, forces):
    pitch = PITCH[0]
    row = lax.broadcasted_iota(jnp.int32, (pitch, CHUNK), 0)
    depth_row = lax.broadcasted_iota(jnp.int32, (NZ, CHUNK), 0)
    for chunk in range(PART // CHUNK):
        part = pl.ds(chunk * CHUNK, CHUNK)
        x = cells_v[0:1, part] & (CX - 1)
        y = cells_v[1:2, part] & (CY - 1)
        z = cells_v[2:3, part]
        fx, fy, fz = offsets_v[0:1, part], offsets_v[1:2, part], offsets_v[2:3, part]
        hot_low = jnp.where(depth_row == column_of(z), 1.0, 0.0).astype(BF16)
        hot_high = jnp.where(depth_row == column_of((z + 1) & (NZ - 1)), 1.0, 0.0).astype(BF16)
        across = jnp.where(row == y, 1.0 - fy, 0.0) + jnp.where(row == y + 1, fy, 0.0)
        across_slope = jnp.where(row == y + 1, 1.0, 0.0) - jnp.where(row == y, 1.0, 0.0)
        first = cells_s[0, chunk * CHUNK] & (CX - 1)
        last = cells_s[0, chunk * CHUNK + CHUNK - 1] & (CX - 1)

        def plane(px, carry):
            rows = pl.ds(pl.multiple_of(px * pitch, 8), 2 * pitch)
            values = jnp.concatenate([field[group, rows, :] for group in range(4)], axis=1)
            high, low = split(values)
            at_low = jnp.dot(high, hot_low, preferred_element_type=F32) + jnp.dot(
                low, hot_low, preferred_element_type=F32
            )
            at_high = jnp.dot(high, hot_high, preferred_element_type=F32) + jnp.dot(
                low, hot_high, preferred_element_type=F32
            )
            value = (1.0 - fz) * at_low + fz * at_high
            change = at_high - at_low
            low_x, high_x = value[:pitch], value[pitch:]
            value_x = (1.0 - fx) * low_x + fx * high_x
            change_x = (1.0 - fx) * change[:pitch] + fx * change[pitch:]
            found = (
                jnp.sum(across * value_x, axis=0, keepdims=True),
                jnp.sum(across * (high_x - low_x), axis=0, keepdims=True),
                jnp.sum(across_slope * value_x, axis=0, keepdims=True),
                jnp.sum(across * change_x, axis=0, keepdims=True),
            )
            here = x == px
            return tuple(jnp.where(here, new, old) for new, old in zip(found, carry))

        nothing = jnp.zeros((1, CHUNK), F32)
        found = lax.fori_loop(first, last + 1, plane, (nothing,) * 4)
        minus = -charges_v[0:1, part]
        potential[0:1, part] = found[0]
        for axis in range(3):
            forces[axis : axis + 1, part] = minus * found[1 + axis]


def depth_sums(values, level):
    if level == 0:
        up0, up1 = turn(values[0], -1), turn(values[1], -1)
        down2, down3 = turn(values[2], 1), turn(values[3], 1)
        one = [down3 + values[1], values[0] + values[2], values[1] + values[3], values[2] + up0]
        two = [down2 + values[2], down3 + values[3], values[0] + up0, values[1] + up1]
        return one, two
    if level == 1:
        up0, up1 = turn(values[0], -1), turn(values[1], -1)
        down0, down1 = turn(values[0], 1), turn(values[1], 1)
        return [down1 + values[1], values[0] + up0], [down0 + up0, down1 + up1]
    step = LANE_STEP[level]
    value = values[0]
    return (
        [turn(value, step) + turn(value, -step)],
        [turn(value, 2 * step) + turn(value, -2 * step)],
    )


def near_depth(level, grid, mixed, first, count):
    pitch = PITCH[level]

    def plane(p, carry):
        rows = pl.ds(pl.multiple_of(p * pitch, 8), pitch)
        values = [grid[group, rows, :] for group in range(GROUPS[level])]
        one, two = depth_sums(values, level)
        for group in range(GROUPS[level]):
            for term in range(TERMS):
                mixed[term, group, rows, :] = (
                    values[group] + NEAR_ONE[term] * one[group] + NEAR_TWO[term] * two[group]
                )
        return carry

    lax.fori_loop(first, first + count, plane, 0)


def near_rest(level, mixed, weights, out, low, high):
    pitch = PITCH[level]
    blocks = -(-(COUNT_Y[level] + 1) // 8)
    scale = [0.5**level * weights[level, term] for term in range(TERMS)]
    scale_one = [scale[t] * NEAR_ONE[t] for t in range(TERMS)]
    scale_two = [scale[t] * NEAR_TWO[t] for t in range(TERMS)]

    def one_block(step, carry):
        group = step // blocks
        start = step % blocks * 8
        zero, one, two = {}, {}, {}
        for plane in range(low, high + 4):
            terms = []
            for term in range(TERMS):
                cells = [
                    mixed[term, group, pl.ds(plane * pitch + start + shift, 8), :]
                    for shift in range(5)
                ]
                terms.append(
                    cells[2]
                    + NEAR_ONE[term] * (cells[1] + cells[3])
                    + NEAR_TWO[term] * (cells[0] + cells[4])
                )
            for table, factors in ((zero, scale), (one, scale_one), (two, scale_two)):
                table[plane] = sum(factors[t] * terms[t] for t in range(1, TERMS)) + factors[0] * terms[0]
            done = plane - 4
            if done >= low:
                out[group, pl.ds(done * pitch + start, 8), :] = (
                    zero[done + 2] + (one[done + 1] + one[done + 3]) + (two[done] + two[done + 4])
                )
        return carry

    lax.fori_loop(0, GROUPS[level] * blocks, one_block, 0)


def halve(level, source, padded, store):
    pitch = PITCH[level]
    groups = GROUPS[level]
    top = COUNT_X[level]
    for plane in range(top // 2 + 1):

        def at(group, p):
            return source[group, pl.ds(p * pitch, pitch), :]

        mixed = []
        for group in range(groups):
            sides = [at(group, p) for p in (2 * plane - 1, 2 * plane + 1) if 0 <= p <= top]
            mixed.append(at(group, 2 * plane) + 0.5 * sum(sides[1:], sides[0]))
        if level == 0:
            halved = [
                mixed[0] + 0.5 * (turn(mixed[3], 1) + mixed[1]),
                mixed[2] + 0.5 * (mixed[1] + mixed[3]),
            ]
        elif level == 1:
            halved = [mixed[0] + 0.5 * (turn(mixed[1], 1) + mixed[1])]
        else:
            halved = [mixed[0] + 0.5 * (turn(mixed[0], 1) + turn(mixed[0], -1))]
        next_pitch = PITCH[level + 1]
        for group, value in enumerate(halved):
            padded[group, 8 : 8 + pitch, :] = value
            result = padded[group, pl.ds(6, next_pitch, stride=2), :] + 0.5 * (
                padded[group, pl.ds(5, next_pitch, stride=2), :]
                + padded[group, pl.ds(7, next_pitch, stride=2), :]
            )
            store(group, plane, result)


def double(level, coarse, fine):
    pitch, coarse_pitch = PITCH[level], PITCH[level + 1]
    count = pitch // 2
    last = None
    for plane in range(COUNT_X[level + 1] + 1):
        now = []
        rows = [
            [coarse[group, pl.ds(plane * coarse_pitch + shift, count), :] for shift in (0, 1)]
            for group in range(GROUPS[level + 1])
        ]
        for values in ([r[0] for r in rows], [0.5 * (r[0] + r[1]) for r in rows]):
            if level == 0:
                v0, v1 = values
                now.append([v0, 0.5 * (v0 + v1), v1, 0.5 * (v1 + turn(v0, -1))])
            elif level == 1:
                now.append([values[0], 0.5 * (values[0] + turn(values[0], -1))])
            else:
                now.append(values)
        for parity in range(2):
            for group in range(GROUPS[level]):
                if last is not None:
                    place = pl.ds((2 * plane - 1) * pitch + parity, count, stride=2)
                    fine[group, place, :] += 0.5 * (last[parity][group] + now[parity][group])
                place = pl.ds(2 * plane * pitch + parity, count, stride=2)
                fine[group, place, :] += now[parity][group]
        last = now


def field_kernel(
    weights,
    screening,
    own0,
    forward_high,
    forward_low,
    back_high,
    back_low,
    out,
    grid0,
    grid1,
    grid2,
    grid3,
    own1,
    own2,
    own3,
    field1,
    field2,
    field3,
    mixed0,
    mixed1,
    mixed2,
    mixed3,
    padded0,
    padded1,
    padded2,
    x0,
    x1,
    x2,
    y_out,
    y_in,
    c_out,
    c_in,
    in3,
    stage1,
    gathered,
    stage2,
    x_send,
    x_recv,
    y_send,
    y_recv,
    c_send,
    c_recv,
    send3,
    recv3,
    send_a,
    recv_a,
    send_b,
    recv_b,
):
    me_x, me_y = lax.axis_index("gx"), lax.axis_index("gy")

    def device(dx, dy):
        return (
            lax.rem(me_x + (dx + N_GX), N_GX) if dx else me_x,
            lax.rem(me_y + (dy + N_GY), N_GY) if dy else me_y,
        )

    peers = [(0, d) for d in range(1, N_GY)] + [(d, 0) for d in range(1, N_GX)]
    peers += [(dx, dy) for dx in (-2, -1, 1, 2) for dy in (-1, 1)]
    barrier = pltpu.get_barrier_semaphore()
    for peer in peers:
        pl.semaphore_signal(barrier, inc=1, device_id=device(*peer), device_id_type=MESH)

    own = (own0, own1, own2, own3)
    grids = (grid0, grid1, grid2, grid3)
    fields = (out, field1, field2, field3)
    mixes = (mixed0, mixed1, mixed2, mixed3)

    padded0[...] = jnp.zeros_like(padded0)
    padded1[...] = jnp.zeros_like(padded1)
    padded2[...] = jnp.zeros_like(padded2)

    def keep(level):
        def store(group, plane, value):
            pitch = PITCH[level]
            own[level][group, pl.ds(plane * pitch, pitch), :] = value
            grids[level][group, pl.ds((plane + 2) * pitch, pitch), :] = value

        return store

    halve(0, own0, padded0, keep(1))
    halve(1, own1, padded1, keep(2))
    grid3[...] = jnp.zeros_like(grid3)

    def keep3(group, plane, value):
        grid3[group, pl.ds((plane + 2) * 16, 16), :] = value
        own3[pl.ds(plane * 8, 8), :] = grid3[group, pl.ds((plane + 2) * 16 + 2, 8), :]

    halve(2, own2, padded2, keep3)
    for side in range(2):
        mixed = (
            own3[0:8, :] + 0.5 * own3[8:16, :] if side == 0 else own3[16:24, :] + 0.5 * own3[8:16, :]
        )
        mixed = mixed + 0.5 * (turn(mixed, 2) + turn(mixed, -2))
        padded2[0, 0:8, :] = jnp.zeros((8, 128), F32)
        padded2[0, 8:16, :] = mixed
        padded2[0, 16:24, :] = jnp.zeros((8, 128), F32)
        result = padded2[0, pl.ds(8, 8, stride=2), :] + 0.5 * (
            padded2[0, pl.ds(7, 8, stride=2), :] + padded2[0, pl.ds(9, 8, stride=2), :]
        )
        stage1[0, pl.ds(4 * side, 4), :] = result[0:4]

    pl.semaphore_wait(barrier, len(peers))

    sends = []

    def send(source, target, send_sem, recv_sem, dx, dy):
        copy = pltpu.make_async_remote_copy(
            src_ref=source,
            dst_ref=target,
            send_sem=send_sem,
            recv_sem=recv_sem,
            device_id=device(dx, dy),
            device_id_type=MESH,
        )
        copy.start()
        sends.append(copy)
        return copy

    copies_a = [
        send(stage1.at[0], stage1.at[d], send_a.at[d], recv_a.at[d], 0, d) for d in range(1, N_GY)
    ]
    for level in range(3):
        count = COUNT_X[level] + 1
        for term in range(3):
            for group in range(GROUPS[level]):
                for side in range(2):
                    y = term if side == 0 else COUNT_Y[level] - 2 + term
                    y_out[side, pl.ds(Y_OFFSET[level, term, group], count), :] = own[level][
                        group, pl.ds(2 + y, count, stride=PITCH[level]), :
                    ]
    copies_y = [
        send(y_out.at[side], y_in.at[1 - side], y_send.at[side], y_recv.at[side], 0, 2 * side - 1)
        for side in range(2)
    ]
    copies_3 = [
        send(own3, in3.at[k], send3.at[k], recv3.at[k], -dx, -dy) for k, (dx, dy) in enumerate(FAR3)
    ]
    for (level, term, group), place in C_OFFSET.items():
        for side_x in range(2):
            start = 0 if side_x == 0 else COUNT_X[level] - 2
            for side_y in range(2):
                c_out[2 * side_x + side_y, pl.ds(place, 3), :] = y_out[
                    side_y, pl.ds(Y_OFFSET[level, term, group] + start, 3), :
                ]
    copies_c = [
        send(
            c_out.at[k],
            c_in.at[3 - k],
            c_send.at[k],
            c_recv.at[k],
            2 * (k // 2) - 1,
            2 * (k % 2) - 1,
        )
        for k in range(4)
    ]
    copies_x = []
    for level, landing in ((2, x2), (1, x1), (0, x0)):
        pitch = PITCH[level]
        for side in range(2):
            start = 0 if side == 0 else (COUNT_X[level] - 2) * pitch
            copies_x.append(
                send(
                    own[level].at[:, pl.ds(start, 3 * pitch), :],
                    landing.at[1 - side],
                    x_send.at[2 * level + side],
                    x_recv.at[2 * level + side],
                    2 * side - 1,
                    0,
                )
            )

    line = lax.broadcasted_iota(jnp.int32, (N_GX, 512), 0)
    column = lax.broadcasted_iota(jnp.int32, (N_GX, 512), 1)
    top_y = ((column >> 5) & 3) * 4 + (column >> 7)
    top_z = column & 31
    far_x = jnp.minimum(line, N_GX - line)
    far_y = jnp.minimum(top_y, 16 - top_y)
    far_z = jnp.minimum(top_z, 32 - top_z)
    squared = (far_x * far_x + far_y * far_y + far_z * far_z).astype(F32)
    kernel = jnp.exp(-screening[0] * jnp.sqrt(squared)) / jnp.sqrt(1.0 + squared)
    kernel_hat = dot3(kernel, forward_high[...], forward_low[...])
    kernel_next = pltpu.roll(kernel_hat, N_GX - 1, 0)

    for copy in copies_a:
        copy.wait_recv()
    for side in range(2):
        for y in range(16):
            slot = (16 - y // 2 * 2) // 2 % 8
            if y % 2:
                value = stage1[slot, pl.ds(4 * side + 1, 1), :]
            else:
                value = (
                    stage1[slot, pl.ds(4 * side, 1), :]
                    + stage1[(slot + 1) % 8, pl.ds(4 * side + 2, 1), :]
                )
            gathered[y // 4, pl.ds(4 * side + y % 4, 1), :] = value
    packed = jnp.concatenate([gathered[q] for q in range(4)], axis=1)
    source = lax.broadcasted_iota(jnp.int32, (512, 128), 0)
    target = lax.broadcasted_iota(jnp.int32, (512, 128), 1)
    place = jnp.where(source == (target >> 5) * 128 + (target & 31) * 4, 1.0, 0.0).astype(BF16)
    packed_high, packed_low = split(packed)
    packed = jnp.dot(packed_high, place, preferred_element_type=F32) + jnp.dot(
        packed_low, place, preferred_element_type=F32
    )
    stage2[pl.ds(0, 8), :] = packed
    stage2[pl.ds(N_GX * 8, 8), :] = packed
    copies_b = [
        send(
            stage2.at[pl.ds(0, 8), :],
            stage2.at[pl.ds(8 * d, 8), :],
            send_b.at[d],
            recv_b.at[d],
            d,
            0,
        )
        for d in range(1, N_GX)
    ]

    grid0[:, pl.ds(2 * PITCH[0], 17 * PITCH[0]), :] = own0[...]
    for level in range(4):
        rows = mixes[level].shape[2]
        for group in range(GROUPS[level]):
            for term in range(TERMS):
                mixes[level][term, group, pl.ds(rows - 8, 8), :] = jnp.zeros((8, 128), F32)
    for copy in copies_y:
        copy.wait_recv()
    for level in range(3):
        pitch, count = PITCH[level], COUNT_X[level] + 1
        for term in range(3):
            for group in range(GROUPS[level]):
                for side in range(2):
                    y = term - 2 if side == 0 else COUNT_Y[level] + term
                    rows = pl.ds(2 * pitch + y + 2, count, stride=pitch)
                    grids[level][group, rows, :] += y_in[
                        side, pl.ds(Y_OFFSET[level, term, group], count), :
                    ]
    near_depth(0, grid0, mixed0, 3, 15)
    near_rest(0, mixed0, weights, out, 3, 14)

    for copy in copies_3:
        copy.wait_recv()
    for k, (dx, dy) in enumerate(FAR3):
        first, count = (2, 3) if dy < 0 else (0, 3) if dy > 0 else (0, 5)
        for plane in range(3):
            x = 2 * dx + plane
            if -2 <= x <= 4:
                rows = pl.ds((x + 2) * 16 + 4 * dy + first + 2, count)
                grid3[0, rows, :] += in3[k, pl.ds(plane * 8 + first, count), :]
    near_depth(3, grid3, mixed3, 0, 7)
    near_rest(3, mixed3, weights, field3, 0, 3)
    lane = lax.broadcasted_iota(jnp.int32, (8, 128), 1)
    for plane in range(3):
        value = field3[0, pl.ds(plane * 16, 8), :]
        field3[0, pl.ds(plane * 16, 8), :] = jnp.where(
            lane % 2 == 0, value, 0.5 * (turn(value, 1) + turn(value, -1))
        )
        field3[0, pl.ds(plane * 16 + 8, 8), :] = jnp.zeros((8, 128), F32)

    for copy in copies_c:
        copy.wait_recv()
    for number, (level, landing) in enumerate(((2, x2), (1, x1), (0, x0))):
        pitch, size_x, grid = PITCH[level], COUNT_X[level], grids[level]
        for copy in copies_x[2 * number : 2 * number + 2]:
            copy.wait_recv()
        grid[:, pl.ds(0, 2 * pitch), :] = landing[0, :, pl.ds(0, 2 * pitch), :]
        grid[:, pl.ds(2 * pitch, pitch), :] += landing[0, :, pl.ds(2 * pitch, pitch), :]
        start = (size_x + 2) * pitch
        grid[:, pl.ds(start, pitch), :] += landing[1, :, pl.ds(0, pitch), :]
        grid[:, pl.ds(start + pitch, 2 * pitch), :] = landing[1, :, pl.ds(pitch, 2 * pitch), :]
        for term in range(3):
            for group in range(GROUPS[level]):
                for k in range(4):
                    x = -2 if k // 2 == 0 else size_x
                    y = term - 2 if k % 2 == 0 else COUNT_Y[level] + term
                    rows = pl.ds((x + 2) * pitch + y + 2, 3, stride=pitch)
                    grid[group, rows, :] += c_in[k, pl.ds(C_OFFSET[level, term, group], 3), :]
        if level:
            near_depth(level, grid, mixes[level], 0, size_x + 5)
            near_rest(level, mixes[level], weights, fields[level], 0, size_x + 1)
        else:
            near_depth(0, grid, mixed0, 0, 3)
            near_depth(0, grid, mixed0, 18, 3)
            near_rest(0, mixed0, weights, out, 0, 3)
            near_rest(0, mixed0, weights, out, 14, 17)

    for copy in copies_b:
        copy.wait_recv()
    planes = jnp.concatenate(
        [
            stage2[pl.ds(r, N_GX, stride=8), :] + stage2[pl.ds(12 + r, N_GX, stride=8), :]
            for r in range(4)
        ],
        axis=1,
    )
    hat = dot3(planes, forward_high[...], forward_low[...])
    low = jnp.sum(kernel_hat * hat, axis=0, keepdims=True)
    high = jnp.sum(kernel_next * hat, axis=0, keepdims=True)
    pair = jnp.concatenate([low, high, jnp.zeros((6, 512), F32)], axis=0)
    top = dot3(pair, back_high[...], back_low[...])
    rows_of = [[top[side : side + 1, b * 128 : b * 128 + 128] for b in range(3)] for side in range(2)]
    for plane in range(3):
        line_of = (
            rows_of[0]
            if plane == 0
            else rows_of[1]
            if plane == 2
            else [0.5 * (rows_of[0][b] + rows_of[1][b]) for b in range(3)]
        )
        for y in range(5):
            value = line_of[y // 2] if y % 2 == 0 else 0.5 * (line_of[y // 2] + line_of[y // 2 + 1])
            field3[0, pl.ds(plane * 16 + y, 1), :] += value
    for level in (2, 1, 0):
        double(level, fields[level + 1], fields[level])
    for copy in sends:
        copy.wait_send()


def transforms():
    def cas(size):
        angle = 2.0 * np.pi * np.outer(np.arange(size), np.arange(size)) / size
        return np.cos(angle) + np.sin(angle)

    cas_y, cas_z = cas(16), cas(32)
    source = np.arange(512)
    source_y = ((source >> 5) & 3) * 4 + (source >> 7)
    source_z = source & 31
    forward = (cas_y[source_y][:, :, None] * cas_z[source_z][:, None, :]).reshape(512, 512)
    lane = np.arange(128)
    share = (lane % 4) / 4.0
    lanes = (1.0 - share) * cas_z[:, lane // 4] + share * cas_z[:, (lane // 4 + 1) % 32]
    back = (cas_y[:, None, :3, None] * lanes[None, :, None, :]).reshape(512, 384)
    back = back * (TOP_WEIGHT / 512.0)

    def pair(values):
        high = values.astype(jnp.bfloat16)
        low = (values - high.astype(np.float64)).astype(jnp.bfloat16)
        return high, low

    return pair(forward) + pair(back)


def local(cells, offsets, charges, kernel_weights, screening):
    charges_row = charges.reshape(1, PART)
    vmem = pl.BlockSpec(memory_space=pltpu.VMEM)
    smem = pl.BlockSpec(memory_space=pltpu.SMEM)
    limit = 48 * 1024 * 1024
    grid_shape = (4, 17 * PITCH[0], 128)
    deposited = pl.pallas_call(
        deposit_kernel,
        out_shape=jax.ShapeDtypeStruct(grid_shape, F32),
        in_specs=[smem, vmem, vmem, vmem],
        out_specs=vmem,
        compiler_params=pltpu.CompilerParams(vmem_limit_bytes=limit),
        name="deposit",
    )(cells, cells, offsets, charges_row)

    def rimmed(level):
        return (GROUPS[level], (COUNT_X[level] + 5) * PITCH[level] + 8, 128)

    scratch = [pltpu.VMEM(rimmed(level), F32) for level in range(4)]
    scratch += [
        pltpu.VMEM((GROUPS[level], (COUNT_X[level] + 1) * PITCH[level], 128), F32) for level in (1, 2)
    ]
    scratch += [pltpu.VMEM((24, 128), F32)]
    scratch += [
        pltpu.VMEM((GROUPS[level], (COUNT_X[level] + 1) * PITCH[level], 128), F32)
        for level in (1, 2, 3)
    ]
    scratch += [pltpu.VMEM((TERMS,) + rimmed(level), F32) for level in range(4)]
    scratch += [pltpu.VMEM((2, 56, 128), F32), pltpu.VMEM((1, 40, 128), F32), pltpu.VMEM((1, 40, 128), F32)]
    scratch += [pltpu.VMEM((2, GROUPS[level], 3 * PITCH[level], 128), F32) for level in range(3)]
    scratch += [pltpu.VMEM((2, Y_ROWS, 128), F32)] * 2
    scratch += [pltpu.VMEM((4, C_ROWS, 128), F32)] * 2
    scratch += [
        pltpu.VMEM((len(FAR3), 24, 128), F32),
        pltpu.VMEM((N_GY, 8, 128), F32),
        pltpu.VMEM((4, 8, 128), F32),
        pltpu.VMEM(((N_GX + 1) * 8, 128), F32),
    ]
    for count in (6, 2, 4, len(FAR3), N_GY, N_GX):
        scratch += [pltpu.SemaphoreType.DMA((count,))] * 2
    field = pl.pallas_call(
        field_kernel,
        out_shape=jax.ShapeDtypeStruct(grid_shape, F32),
        in_specs=[smem, smem] + [vmem] * 5,
        out_specs=vmem,
        scratch_shapes=scratch,
        compiler_params=pltpu.CompilerParams(
            vmem_limit_bytes=limit, collective_id=0, has_side_effects=True
        ),
        name="field",
    )(kernel_weights, screening, deposited, *[jnp.asarray(t) for t in transforms()])
    potential, forces = pl.pallas_call(
        sample_kernel,
        out_shape=[
            jax.ShapeDtypeStruct((1, PART), F32),
            jax.ShapeDtypeStruct((3, PART), F32),
        ],
        in_specs=[smem] + [vmem] * 4,
        out_specs=[vmem, vmem],
        compiler_params=pltpu.CompilerParams(vmem_limit_bytes=limit),
        name="sample",
    )(cells, cells, offsets, charges_row, field)
    return (potential.reshape(PART), forces)


def solution(mesh):
    return jax.shard_map(
        local,
        mesh=mesh,
        in_specs=(P(None, ("gx", "gy")), P(None, ("gx", "gy")), P(("gx", "gy")), P(), P()),
        out_specs=(P(("gx", "gy")), P(None, ("gx", "gy"))),
        check_vma=False,
    )
```

profile of v0, /device:TPU:2, one launch (start us, length us, event | category | flops | bytes accessed | tf_op | source)
XLA Modules:
  0.0 56.8 jit_solution(11032314871820918098)
XLA Ops:
  0.6 0.0 copy-start
  0.6 0.0 copy-start.1
  1.4 0.0 copy-start.2
  1.4 0.7 %copy-done.2 = s32[3,2048]{1,0:T(4,128)S(1)} copy-done((s32[3,2048]{1,0:T(4,128)S(1)}, s32[3,2048]{1,0:T(4,128)}, u32[]{:S(2)}) %copy-start.2) | copy-done | bytes 24600
  2.1 0.0 copy-start.5
  2.1 0.8 %copy-done.5 = f32[3,2048]{1,0:T(4,128)S(1)} copy-done((f32[3,2048]{1,0:T(4,128)S(1)}, f32[3,2048]{1,0:T(4,128)}, u32[]{:S(2)}) %copy-start.5) | copy-done | bytes 24600
  2.9 0.0 copy-start.6
  2.9 0.7 %copy-done.6 = f32[2048]{0:T(1024)S(1)} copy-done((f32[2048]{0:T(1024)S(1)}, f32[2048]{0:T(1024)}, u32[]{:S(2)}) %copy-start.6) | copy-done | bytes 8216
  3.6 0.0 copy-start.3
  3.6 0.0 copy-start.8
  3.6 11.0 %deposit.1.own0 = f32[4,680,128]{2,1,0:T(8,128)S(1)} custom-call(s32[3,2048]{1,0:T(4,128)S(1)} %copy-done.2, s32[3,2048]{1,0:T(4,128)S(1)} %copy-done.2, f32[3,2048]{1,0:T(4,128)S(1)} %copy-done.5, f32[1,2048]{1,0:T(1,128)S(1)} %bitcast.2), custom_call_target="tpu_custom_call" | custom-call | tf_op jit(solution)/shard_map/deposit/pallas_call | solution.py:641
  14.6 0.0 copy-done
  14.6 0.0 copy-done.1
  14.6 0.0 copy-done.3
  14.6 0.0 copy-done.8
  14.7 0.0 copy-start.4
  14.7 1.0 %copy-done.4 = bf16[512,384]{1,0:T(8,128)(2,1)S(1)} copy-done((bf16[512,384]{1,0:T(8,128)(2,1)S(1)}, bf16[512,384]{1,0:T(8,128)(2,1)}, u32[]{:S(2)}) %copy-start.4) | copy-done | bytes 393240
  15.7 0.0 copy-start.7
  15.7 30.1 %field.1 = f32[4,680,128]{2,1,0:T(8,128)S(1)} custom-call(f32[4,3]{1,0:T(4,128)S(1)} %copy-done.8, f32[1]{0:T(128)S(6)} %copy.11.screening, f32[4,680,128]{2,1,0:T(8,128)S(1)} %deposit.1.own0, bf16[512,512]{1,0:T(8,128)(2,1)S(1)} %copy-done.1, bf16[512,512]{1,0:T(8,128)(2,1)S(1)} %copy-done, bf16[512,384]{1,0:T(8,128)(2,1)S(1)} %copy-done.4, ...), custom_call_target="tpu_custom_call" | custom-call | tf_op jit(solution)/shard_map/field/pallas_call | solution.py:675
  45.8 0.0 copy-done.7
  45.8 10.9 %sample.1 = (f32[1,2048]{1,0:T(1,128)}, f32[3,2048]{1,0:T(4,128)}) custom-call(s32[3,2048]{1,0:T(4,128)S(1)} %copy-done.2, s32[3,2048]{1,0:T(4,128)S(1)} %copy-done.2, f32[3,2048]{1,0:T(4,128)S(1)} %copy-done.5, f32[1,2048]{1,0:T(1,128)S(1)} %bitcast.3, f32[4,680,128]{2,1,0:T(8,128)S(1)} %field.1), custom_call_target="tpu_custom_call" | custom-call | tf_op jit(solution)/shard_map/sample/pallas_call | solution.py:686
Async XLA Ops:
  0.6 14.0 %copy-start = (bf16[512,512]{1,0:T(8,128)(2,1)S(1)}, bf16[512,512]{1,0:T(8,128)(2,1)}, u32[]{:S(2)}) copy-start(bf16[512,512]{1,0:T(8,128)(2,1)} %constant.9.clone.forward_low) | copy-start | bytes 1572868
  0.6 14.0 %copy-start.1 = (bf16[512,512]{1,0:T(8,128)(2,1)S(1)}, bf16[512,512]{1,0:T(8,128)(2,1)}, u32[]{:S(2)}) copy-start(bf16[512,512]{1,0:T(8,128)(2,1)} %constant.8.clone.forward_high) | copy-start | bytes 1572868
  1.4 0.8 %copy-start.2 = (s32[3,2048]{1,0:T(4,128)S(1)}, s32[3,2048]{1,0:T(4,128)}, u32[]{:S(2)}) copy-start(s32[3,2048]{1,0:T(4,128)} %cells_v.3) | copy-start | bytes 73732
  2.1 0.8 %copy-start.5 = (f32[3,2048]{1,0:T(4,128)S(1)}, f32[3,2048]{1,0:T(4,128)}, u32[]{:S(2)}) copy-start(f32[3,2048]{1,0:T(4,128)} %offsets_v.3) | copy-start | bytes 73732
  2.9 0.7 %copy-start.6 = (f32[2048]{0:T(1024)S(1)}, f32[2048]{0:T(1024)}, u32[]{:S(2)}) copy-start(f32[2048]{0:T(1024)} %param.11) | copy-start | bytes 24580
  3.6 11.0 %copy-start.3 = (bf16[512,384]{1,0:T(8,128)(2,1)S(1)}, bf16[512,384]{1,0:T(8,128)(2,1)}, u32[]{:S(2)}) copy-start(bf16[512,384]{1,0:T(8,128)(2,1)} %constant.11.clone.back_low) | copy-start | bytes 1179652
  3.6 11.0 %copy-start.8 = (f32[4,3]{1,0:T(4,128)S(1)}, f32[4,3]{1,0:T(4,128)}, u32[]{:S(2)}) copy-start(f32[4,3]{1,0:T(4,128)} %weights.1) | copy-start | bytes 148
  14.7 1.0 %copy-start.4 = (bf16[512,384]{1,0:T(8,128)(2,1)S(1)}, bf16[512,384]{1,0:T(8,128)(2,1)}, u32[]{:S(2)}) copy-start(bf16[512,384]{1,0:T(8,128)(2,1)} %constant.10.clone.back_high) | copy-start | bytes 1179652
  15.7 30.2 %copy-start.7 = (f32[2048]{0:T(1024)S(1)}, f32[2048]{0:T(1024)}, u32[]{:S(2)}) copy-start(f32[2048]{0:T(1024)} %param.11) | copy-start | bytes 24580
where the time goes:
time: 57.8 us; the launch traced here: 56.8 us
  Pallas kernels  52.1 us (90%)
  local copies, waits for them, and re-layouts  3.22 us (6%)
  between operations  1.45 us (3%)
    pallas_call x1, Pallas kernels, local(): pl.pallas_call(field_kernel, out_shape=jax.ShapeDtypeStruct(grid_shape, F...  30.1 us
    pallas_call x1, Pallas kernels, local(): pl.pallas_call(deposit_kernel, out_shape=jax.ShapeDtypeStruct(grid_shape,...  11 us
    pallas_call x1, Pallas kernels, local(): pl.pallas_call(sample_kernel, out_shape=[jax.ShapeDtypeStruct((1, PART),...  10.9 us
    unnamed x18, local copies, waits for them, and re-layouts  3.22 us

commit v1 on v0

--- a/solution.py
+++ b/solution.py
@@ -62,100 +62,105 @@
     return (depth & 3) * 128 + (depth >> 2)
 
 
-def deposit_kernel(cells_s, cells_v, offsets_v, charges_v, out_ref):
-    out_ref[...] = jnp.zeros_like(out_ref)
+def load_particles(hbm, vmem, sems):
+    copies = [pltpu.make_async_copy(h, v, sems.at[k]) for k, (h, v) in enumerate(zip(hbm, vmem))]
+    for copy in copies:
+        copy.start()
+    return copies
+
+
+def plane_spans(cells_v, *lead):
+    spans = []
+    for chunk in range(PART // CHUNK):
+        part = slice(chunk * CHUNK, (chunk + 1) * CHUNK)
+        x = (cells_v[(*lead, slice(0, 1), part)] & (CX - 1)).astype(F32)
+        spans.append((jnp.min(x).astype(jnp.int32), jnp.max(x).astype(jnp.int32)))
+    return spans
+
+
+def further_windows(spans, starts_of, width, span_s, visit):
+    for chunk, (first, last) in enumerate(spans):
+        span_s[2 * chunk] = starts_of(first) + width
+        span_s[2 * chunk + 1] = last + 1
+
+    def one_chunk(chunk, carry):
+        start, end = span_s[2 * chunk], span_s[2 * chunk + 1]
+
+        def one_window(step, inner):
+            visit(pl.multiple_of(chunk * CHUNK, CHUNK), start + step * width)
+            return inner
+
+        windows = lax.div(jnp.maximum(end - start + width, 0), width)
+        return lax.fori_loop(0, windows, one_window, carry)
+
+    lax.fori_loop(0, PART // CHUNK, one_chunk, 0)
+
+
+DEPOSIT_PLANES = 5
+SAMPLE_PLANES = 6
+
+
+HALO_PLANES = 3
+HALO_CHUNKS = 2
+
+
+def spread(cells, offsets, charge, base, start, width):
     pitch = PITCH[0]
     row = lax.broadcasted_iota(jnp.int32, (pitch, CHUNK), 0)
     depth_row = lax.broadcasted_iota(jnp.int32, (NZ, CHUNK), 0)
-    for chunk in range(PART // CHUNK):
-        part = pl.ds(chunk * CHUNK, CHUNK)
-        x = cells_v[0:1, part] & (CX - 1)
-        y = (cells_v[1:2, part] & (CY - 1)) + 2
-        z = cells_v[2:3, part]
-        fx, fy, fz = offsets_v[0:1, part], offsets_v[1:2, part], offsets_v[2:3, part]
-        charge = charges_v[0:1, part]
-        hot = jnp.where(depth_row == column_of(z), 1.0, 0.0).astype(BF16)
-        across = jnp.where(row == y, 1.0 - fy, 0.0) + jnp.where(row == y + 1, fy, 0.0)
-        first = cells_s[0, chunk * CHUNK] & (CX - 1)
-        last = cells_s[0, chunk * CHUNK + CHUNK - 1] & (CX - 1)
-
-        def plane(px, carry):
-            here = jnp.where(x == px, charge, 0.0)
-            low, high = here * (1.0 - fx), here * fx
-            table = jnp.concatenate(
-                [
-                    across * (low * (1.0 - fz)),
-                    across * (high * (1.0 - fz)),
-                    across * (low * fz),
-                    across * (high * fz),
-                ],
-                axis=0,
-            )
-            table_high, table_low = split(table)
-            dims = (((1,), (1,)), ((), ()))
-            spread = lax.dot_general(
-                table_high, hot, dims, preferred_element_type=F32
-            ) + lax.dot_general(table_low, hot, dims, preferred_element_type=F32)
-            rows = pl.ds(pl.multiple_of(px * pitch, 8), 2 * pitch)
-            for group in range(4):
-                value = spread[: 2 * pitch, group * 128 : group * 128 + 128]
-                if group:
-                    above = spread[2 * pitch :, group * 128 - 128 : group * 128]
-                else:
-                    above = turn(spread[2 * pitch :, 384:512], 1)
-                out_ref[group, rows, :] += value + above
-            return carry
-
-        lax.fori_loop(first, last + 1, plane, 0)
-
-
-def sample_kernel(cells_s, cells_v, offsets_v, charges_v, field, potential, forces):
-    pitch = PITCH[0]
-    row = lax.broadcasted_iota(jnp.int32, (pitch, CHUNK), 0)
-    depth_row = lax.broadcasted_iota(jnp.int32, (NZ, CHUNK), 0)
-    for chunk in range(PART // CHUNK):
-        part = pl.ds(chunk * CHUNK, CHUNK)
-        x = cells_v[0:1, part] & (CX - 1)
-        y = cells_v[1:2, part] & (CY - 1)
-        z = cells_v[2:3, part]
-        fx, fy, fz = offsets_v[0:1, part], offsets_v[1:2, part], offsets_v[2:3, part]
-        hot_low = jnp.where(depth_row == column_of(z), 1.0, 0.0).astype(BF16)
-        hot_high = jnp.where(depth_row == column_of((z + 1) & (NZ - 1)), 1.0, 0.0).astype(BF16)
-        across = jnp.where(row == y, 1.0 - fy, 0.0) + jnp.where(row == y + 1, fy, 0.0)
-        across_slope = jnp.where(row == y + 1, 1.0, 0.0) - jnp.where(row == y, 1.0, 0.0)
-        first = cells_s[0, chunk * CHUNK] & (CX - 1)
-        last = cells_s[0, chunk * CHUNK + CHUNK - 1] & (CX - 1)
-
-        def plane(px, carry):
-            rows = pl.ds(pl.multiple_of(px * pitch, 8), 2 * pitch)
-            values = jnp.concatenate([field[group, rows, :] for group in range(4)], axis=1)
-            high, low = split(values)
-            at_low = jnp.dot(high, hot_low, preferred_element_type=F32) + jnp.dot(
-                low, hot_low, preferred_element_type=F32
-            )
-            at_high = jnp.dot(high, hot_high, preferred_element_type=F32) + jnp.dot(
-                low, hot_high, preferred_element_type=F32
-            )
-            value = (1.0 - fz) * at_low + fz * at_high
-            change = at_high - at_low
-            low_x, high_x = value[:pitch], value[pitch:]
-            value_x = (1.0 - fx) * low_x + fx * high_x
-            change_x = (1.0 - fx) * change[:pitch] + fx * change[pitch:]
-            found = (
-                jnp.sum(across * value_x, axis=0, keepdims=True),
-                jnp.sum(across * (high_x - low_x), axis=0, keepdims=True),
-                jnp.sum(across_slope * value_x, axis=0, keepdims=True),
-                jnp.sum(across * change_x, axis=0, keepdims=True),
-            )
-            here = x == px
-            return tuple(jnp.where(here, new, old) for new, old in zip(found, carry))
-
-        nothing = jnp.zeros((1, CHUNK), F32)
-        found = lax.fori_loop(first, last + 1, plane, (nothing,) * 4)
-        minus = -charges_v[0:1, part]
-        potential[0:1, part] = found[0]
-        for axis in range(3):
-            forces[axis : axis + 1, part] = minus * found[1 + axis]
+    plane = lax.broadcasted_iota(jnp.int32, (8, CHUNK), 0) + base
+    x = cells[0] & (CX - 1)
+    y = (cells[1] & (CY - 1)) + 2
+    fx, fy, fz = offsets
+    hot = jnp.where(depth_row == column_of(cells[2]), 1.0, 0.0).astype(BF16)
+    across = jnp.where(row == y, 1.0 - fy, 0.0) + jnp.where(row == y + 1, fy, 0.0)
+    share = jnp.where(plane == x, charge * (1.0 - fx), jnp.where(plane == x + 1, charge * fx, 0.0))
+    share = jnp.where(plane >= start, share, 0.0)
+    shares = (share * (1.0 - fz), share * fz)
+    table = jnp.concatenate(
+        [across * shares[side][k : k + 1] for side in range(2) for k in range(width)], axis=0
+    )
+    high, low = split(table)
+    dims = (((1,), (1,)), ((), ()))
+    total = lax.dot_general(high, hot, dims, preferred_element_type=F32) + lax.dot_general(
+        low, hot, dims, preferred_element_type=F32
+    )
+    count = width * pitch
+    values = []
+    for group in range(4):
+        if group:
+            above = total[count:, group * 128 - 128 : group * 128]
+        else:
+            above = turn(total[count:, 384:512], 1)
+        values.append(total[:count, group * 128 : group * 128 + 128] + above)
+    return values
+
+
+def rows_of(ref, part, *lead):
+    return [ref[(*lead, slice(k, k + 1), part)] for k in range(3)]
+
+
+def deposit_kernel(cells_h, offsets_h, charges_h, out_ref, cells_v, offsets_v, charges_v, span_s, sems):
+    copies = load_particles((cells_h, offsets_h, charges_h), (cells_v, offsets_v, charges_v), sems)
+    out_ref[...] = jnp.zeros_like(out_ref)
+    for copy in copies:
+        copy.wait()
+    pitch, width = PITCH[0], DEPOSIT_PLANES
+
+    def visit(place, start):
+        part = pl.ds(place, CHUNK)
+        base = jnp.minimum(start, CX + 1 - width)
+        values = spread(
+            rows_of(cells_v, part), rows_of(offsets_v, part), charges_v[0:1, part], base, start, width
+        )
+        rows = pl.ds(pl.multiple_of(base * pitch, 8), width * pitch)
+        for group in range(4):
+            out_ref[group, rows, :] += values[group]
+
+    spans = plane_spans(cells_v)
+    for chunk, (first, _) in enumerate(spans):
+        visit(chunk * CHUNK, first)
+    further_windows(spans, lambda first: first, width, span_s, visit)
 
 
 def depth_sums(values, level):
@@ -194,7 +199,14 @@
     lax.fori_loop(first, first + count, plane, 0)
 
 
-def near_rest(level, mixed, weights, out, low, high):
+def near_tail(level, mixed):
+    rows = mixed.shape[2]
+    for group in range(GROUPS[level]):
+        for term in range(TERMS):
+            mixed[term, group, pl.ds(rows - 8, 8), :] = jnp.zeros((8, 128), F32)
+
+
+def near_rest(level, mixed, weights, out, low, high, shift_out=0):
     pitch = PITCH[level]
     blocks = -(-(COUNT_Y[level] + 1) // 8)
     scale = [0.5**level * weights[level, term] for term in range(TERMS)]
@@ -221,12 +233,32 @@
                 table[plane] = sum(factors[t] * terms[t] for t in range(1, TERMS)) + factors[0] * terms[0]
             done = plane - 4
             if done >= low:
-                out[group, pl.ds(done * pitch + start, 8), :] = (
+                out[group, pl.ds((done + shift_out) * pitch + start, 8), :] = (
                     zero[done + 2] + (one[done + 1] + one[done + 3]) + (two[done] + two[done + 4])
                 )
         return carry
 
     lax.fori_loop(0, GROUPS[level] * blocks, one_block, 0)
+
+
+def near_pair(table_high, table_low, cells_high, cells_low, start):
+    rows = pl.ds(start, 6 * PITCH[0])
+    high = cells_high[rows, :]
+    parts = (
+        jnp.dot(table_high[...], high, preferred_element_type=F32)
+        + jnp.dot(table_low[...], high, preferred_element_type=F32)
+        + jnp.dot(table_high[...], cells_low[rows, :], preferred_element_type=F32)
+    )
+    count = 2 * PITCH[0]
+    zero, one, two = [
+        [parts[p * count : (p + 1) * count, g * 128 : g * 128 + 128] for g in range(4)] for p in range(3)
+    ]
+    return [
+        zero[0] + (turn(one[3], 1) + one[1]) + (turn(two[2], 1) + two[2]),
+        zero[1] + (one[0] + one[2]) + (turn(two[3], 1) + two[3]),
+        zero[2] + (one[1] + one[3]) + (two[0] + turn(two[0], -1)),
+        zero[3] + (one[2] + turn(one[0], -1)) + (two[1] + turn(two[1], -1)),
+    ]
 
 
 def halve(level, source, padded, store):
@@ -289,33 +321,206 @@
         last = now
 
 
+def sample_kernel(
+    cells_h,
+    offsets_h,
+    charges_h,
+    near,
+    coarse,
+    grid,
+    table_high,
+    table_low,
+    beside_cells,
+    beside_offsets,
+    beside_charges,
+    potential,
+    forces,
+    cells_v,
+    offsets_v,
+    charges_v,
+    field,
+    edge,
+    edge_high,
+    edge_low,
+    high_v,
+    low_v,
+    span_s,
+    sems,
+):
+    copies = load_particles((cells_h, offsets_h, charges_h), (cells_v, offsets_v, charges_v), sems)
+    pitch, width = PITCH[0], SAMPLE_PLANES
+
+    for side in range(2):
+        count = (8 - side) * pitch
+        edge[side, :, pl.ds(0, count), :] = grid[:, pl.ds(side * 14 * pitch, count), :]
+        if side:
+            edge[side, :, pl.ds(count, pitch), :] = jnp.zeros((4, pitch, 128), F32)
+        target = 4 * side * pitch
+        base = CX - 2 if side == 0 else 0
+
+        def visit(chunk):
+            part = pl.ds(pl.multiple_of(chunk * CHUNK, CHUNK), CHUNK)
+            values = spread(
+                rows_of(beside_cells, part, side),
+                rows_of(beside_offsets, part, side),
+                beside_charges[side, 0:1, part],
+                base,
+                base,
+                HALO_PLANES,
+            )
+            for group in range(4):
+                edge[side, group, pl.ds(target, HALO_PLANES * pitch), :] += values[group]
+
+        chunks = PART // CHUNK
+        spans = plane_spans(beside_cells, side)
+        if side == 0:
+            own_chunks = range(chunks - HALO_CHUNKS, chunks)
+            passed = sum((last < CX - 3).astype(jnp.int32) for _, last in spans)
+            low, high = passed, chunks - HALO_CHUNKS
+        else:
+            own_chunks = range(HALO_CHUNKS)
+            reached = sum((first < 3).astype(jnp.int32) for first, _ in spans)
+            low, high = HALO_CHUNKS, reached
+        for chunk in own_chunks:
+            visit(chunk)
+
+        def more(chunk, carry):
+            visit(chunk)
+            return carry
+
+        lax.fori_loop(low, high, more, 0)
+        for group in range(4):
+            high, low = split(edge[side, group])
+            edge_high[side, :, group * 128 : group * 128 + 128] = high
+            edge_low[side, :, group * 128 : group * 128 + 128] = low
+        for window in range(2):
+            values = near_pair(
+                table_high, table_low, edge_high.at[side], edge_low.at[side], window * 2 * pitch
+            )
+            planes = 1 if side and window else 2
+            for group in range(4):
+                field[group, pl.ds((14 * side + 2 * window) * pitch, planes * pitch), :] = values[group][
+                    : planes * pitch
+                ]
+    field[:, pl.ds(4 * pitch, 10 * pitch), :] = near[:, pl.ds(4 * pitch, 10 * pitch), :]
+    double(0, coarse, field)
+
+    for group in range(5):
+        values = field[group] if group < 4 else turn(field[0], -1)
+        values = jnp.concatenate([values, jnp.zeros((pitch, 128), F32)], axis=0)
+        high, low = split(values)
+        high_v[:, group * 128 : group * 128 + 128] = high
+        low_v[:, group * 128 : group * 128 + 128] = low
+    for copy in copies:
+        copy.wait()
+    row = lax.broadcasted_iota(jnp.int32, (8, CHUNK), 0)
+    depth_row = lax.broadcasted_iota(jnp.int32, (NZ, CHUNK), 0)
+
+    def found_in(place, start):
+        part = pl.ds(place, CHUNK)
+        x = cells_v[0:1, part] & (CX - 1)
+        y = cells_v[1:2, part] & (CY - 1)
+        z = cells_v[2:3, part]
+        fx, fy, fz = offsets_v[0:1, part], offsets_v[1:2, part], offsets_v[2:3, part]
+        hot = jnp.where(depth_row == column_of(z), 1.0, 0.0).astype(BF16)
+        base = jnp.minimum(start, CX + 2 - width)
+        rows = pl.ds(pl.multiple_of(base * pitch, 16), width * pitch)
+        at_low = jnp.dot(high_v[rows, 0:512], hot, preferred_element_type=F32) + jnp.dot(
+            low_v[rows, 0:512], hot, preferred_element_type=F32
+        )
+        at_high = jnp.dot(high_v[rows, 128:640], hot, preferred_element_type=F32) + jnp.dot(
+            low_v[rows, 128:640], hot, preferred_element_type=F32
+        )
+        sums = [jnp.zeros((8, CHUNK), F32)] * 4
+        for k in range(width):
+            picks = []
+            for values in (at_low, at_high):
+                for side in range(2):
+                    pick = jnp.zeros((8, CHUNK), F32)
+                    for block in range(pitch // 8):
+                        start_row = k * pitch + block * 8
+                        pick = jnp.where(row + block * 8 == y + side, values[start_row : start_row + 8], pick)
+                    picks.append(pick)
+            change0, change1 = picks[2] - picks[0], picks[3] - picks[1]
+            value0, value1 = picks[0] + fz * change0, picks[1] + fz * change1
+            value = (1.0 - fy) * value0 + fy * value1
+            change = (1.0 - fy) * change0 + fy * change1
+            plane = base + k
+            on = plane >= start
+            share = jnp.where((x == plane) & on, 1.0 - fx, jnp.where((x + 1 == plane) & on, fx, 0.0))
+            slope = jnp.where((x == plane) & on, -1.0, jnp.where((x + 1 == plane) & on, 1.0, 0.0))
+            sums = [
+                sums[0] + share * value,
+                sums[1] + slope * value,
+                sums[2] + share * (value1 - value0),
+                sums[3] + share * change,
+            ]
+        return [jnp.sum(total, axis=0, keepdims=True) for total in sums]
+
+    def first_visit(place, start):
+        part = pl.ds(place, CHUNK)
+        found = found_in(place, start)
+        minus = -charges_v[0:1, part]
+        potential[0:1, part] = found[0]
+        for axis in range(3):
+            forces[axis : axis + 1, part] = minus * found[1 + axis]
+
+    def visit(place, start):
+        part = pl.ds(place, CHUNK)
+        found = found_in(place, start)
+        minus = -charges_v[0:1, part]
+        potential[0:1, part] += found[0]
+        for axis in range(3):
+            forces[axis : axis + 1, part] += minus * found[1 + axis]
+
+    spans = plane_spans(cells_v)
+    for chunk, (first, _) in enumerate(spans):
+        first_visit(chunk * CHUNK, first & -2)
+    further_windows(spans, lambda first: first & -2, width, span_s, visit)
+
+
 def field_kernel(
     weights,
     screening,
     own0,
+    cells_h,
+    offsets_h,
+    charges_h,
+    forward_high_h,
+    forward_low_h,
+    back_high_h,
+    back_low_h,
+    tables_h,
+    out,
+    field1,
+    grid0,
+    table_high,
+    table_low,
+    beside_cells,
+    beside_offsets,
+    beside_charges,
     forward_high,
     forward_low,
     back_high,
     back_low,
-    out,
-    grid0,
+    tables,
+    cells_high,
+    cells_low,
+    load_sems,
     grid1,
     grid2,
     grid3,
     own1,
     own2,
     own3,
-    field1,
     field2,
     field3,
-    mixed0,
     mixed1,
     mixed2,
     mixed3,
     padded0,
     padded1,
     padded2,
-    x0,
     x1,
     x2,
     y_out,
@@ -326,6 +531,8 @@
     stage1,
     gathered,
     stage2,
+    p_send,
+    p_recv,
     x_send,
     x_recv,
     y_send,
@@ -353,10 +560,25 @@
     for peer in peers:
         pl.semaphore_signal(barrier, inc=1, device_id=device(*peer), device_id_type=MESH)
 
+    loads = [
+        pltpu.make_async_copy(h, v, load_sems.at[k])
+        for k, (h, v) in enumerate(
+            (
+                (forward_high_h, forward_high),
+                (forward_low_h, forward_low),
+                (back_high_h, back_high),
+                (back_low_h, back_low),
+                (tables_h, tables),
+            )
+        )
+    ]
+    for load in loads:
+        load.start()
+
     own = (own0, own1, own2, own3)
     grids = (grid0, grid1, grid2, grid3)
     fields = (out, field1, field2, field3)
-    mixes = (mixed0, mixed1, mixed2, mixed3)
+    mixes = (None, mixed1, mixed2, mixed3)
 
     padded0[...] = jnp.zeros_like(padded0)
     padded1[...] = jnp.zeros_like(padded1)
@@ -395,6 +617,9 @@
     pl.semaphore_wait(barrier, len(peers))
 
     sends = []
+
+    def far_rows(dx):
+        return pl.ds(16, 8) if dx == -2 else pl.ds(0, 8) if dx == 2 else pl.ds(0, 24)
 
     def send(source, target, send_sem, recv_sem, dx, dy):
         copy = pltpu.make_async_remote_copy(
@@ -411,6 +636,23 @@
 
     copies_a = [
         send(stage1.at[0], stage1.at[d], send_a.at[d], recv_a.at[d], 0, d) for d in range(1, N_GY)
+    ]
+    particles = (
+        (cells_h, beside_cells),
+        (offsets_h, beside_offsets),
+        (charges_h, beside_charges),
+    )
+    copies_p = [
+        send(
+            source,
+            landing.at[1 - side],
+            p_send.at[3 * side + k],
+            p_recv.at[3 * side + k],
+            2 * side - 1,
+            0,
+        )
+        for k, (source, landing) in enumerate(particles)
+        for side in range(2)
     ]
     for level in range(3):
         count = COUNT_X[level] + 1
@@ -426,7 +668,8 @@
         for side in range(2)
     ]
     copies_3 = [
-        send(own3, in3.at[k], send3.at[k], recv3.at[k], -dx, -dy) for k, (dx, dy) in enumerate(FAR3)
+        send(own3.at[far_rows(dx)], in3.at[k, far_rows(dx)], send3.at[k], recv3.at[k], -dx, -dy)
+        for k, (dx, dy) in enumerate(FAR3)
     ]
     for (level, term, group), place in C_OFFSET.items():
         for side_x in range(2):
@@ -447,7 +690,7 @@
         for k in range(4)
     ]
     copies_x = []
-    for level, landing in ((2, x2), (1, x1), (0, x0)):
+    for level, landing in ((2, x2), (1, x1)):
         pitch = PITCH[level]
         for side in range(2):
             start = 0 if side == 0 else (COUNT_X[level] - 2) * pitch
@@ -455,8 +698,8 @@
                 send(
                     own[level].at[:, pl.ds(start, 3 * pitch), :],
                     landing.at[1 - side],
-                    x_send.at[2 * level + side],
-                    x_recv.at[2 * level + side],
+                    x_send.at[2 * level - 2 + side],
+                    x_recv.at[2 * level - 2 + side],
                     2 * side - 1,
                     0,
                 )
@@ -471,7 +714,14 @@
     far_z = jnp.minimum(top_z, 32 - top_z)
     squared = (far_x * far_x + far_y * far_y + far_z * far_z).astype(F32)
     kernel = jnp.exp(-screening[0] * jnp.sqrt(squared)) / jnp.sqrt(1.0 + squared)
+    for load in loads[:2]:
+        load.wait()
     kernel_hat = dot3(kernel, forward_high[...], forward_low[...])
+    loads[4].wait()
+    table = weights[0, 0] * tables[0] + weights[0, 1] * tables[1] + weights[0, 2] * tables[2]
+    high, low = split(table)
+    table_high[...] = high
+    table_low[...] = low
     kernel_next = pltpu.roll(kernel_hat, N_GX - 1, 0)
 
     for copy in copies_a:
@@ -509,12 +759,11 @@
         for d in range(1, N_GX)
     ]
 
+    for start, count in ((0, 2), (19, 2)):
+        grid0[:, pl.ds(start * PITCH[0], count * PITCH[0]), :] = jnp.zeros((4, count * PITCH[0], 128), F32)
     grid0[:, pl.ds(2 * PITCH[0], 17 * PITCH[0]), :] = own0[...]
-    for level in range(4):
-        rows = mixes[level].shape[2]
-        for group in range(GROUPS[level]):
-            for term in range(TERMS):
-                mixes[level][term, group, pl.ds(rows - 8, 8), :] = jnp.zeros((8, 128), F32)
+    for level in range(1, 4):
+        near_tail(level, mixes[level])
     for copy in copies_y:
         copy.wait_recv()
     for level in range(3):
@@ -527,8 +776,14 @@
                     grids[level][group, rows, :] += y_in[
                         side, pl.ds(Y_OFFSET[level, term, group], count), :
                     ]
-    near_depth(0, grid0, mixed0, 3, 15)
-    near_rest(0, mixed0, weights, out, 3, 14)
+    for group in range(4):
+        high, low = split(grid0[group, pl.ds(4 * PITCH[0], 14 * PITCH[0]), :])
+        cells_high[:, group * 128 : group * 128 + 128] = high
+        cells_low[:, group * 128 : group * 128 + 128] = low
+    for window in range(5):
+        values = near_pair(table_high, table_low, cells_high, cells_low, window * 2 * PITCH[0])
+        for group in range(4):
+            out[group, pl.ds((4 + 2 * window) * PITCH[0], 2 * PITCH[0]), :] = values[group]
 
     for copy in copies_3:
         copy.wait_recv()
@@ -551,7 +806,18 @@
 
     for copy in copies_c:
         copy.wait_recv()
-    for number, (level, landing) in enumerate(((2, x2), (1, x1), (0, x0))):
+
+    def add_corners(level):
+        for term in range(3):
+            for group in range(GROUPS[level]):
+                for k in range(4):
+                    x = -2 if k // 2 == 0 else COUNT_X[level]
+                    y = term - 2 if k % 2 == 0 else COUNT_Y[level] + term
+                    rows = pl.ds((x + 2) * PITCH[level] + y + 2, 3, stride=PITCH[level])
+                    grids[level][group, rows, :] += c_in[k, pl.ds(C_OFFSET[level, term, group], 3), :]
+
+    add_corners(0)
+    for number, (level, landing) in enumerate(((2, x2), (1, x1))):
         pitch, size_x, grid = PITCH[level], COUNT_X[level], grids[level]
         for copy in copies_x[2 * number : 2 * number + 2]:
             copy.wait_recv()
@@ -560,21 +826,9 @@
         start = (size_x + 2) * pitch
         grid[:, pl.ds(start, pitch), :] += landing[1, :, pl.ds(0, pitch), :]
         grid[:, pl.ds(start + pitch, 2 * pitch), :] = landing[1, :, pl.ds(pitch, 2 * pitch), :]
-        for term in range(3):
-            for group in range(GROUPS[level]):
-                for k in range(4):
-                    x = -2 if k // 2 == 0 else size_x
-                    y = term - 2 if k % 2 == 0 else COUNT_Y[level] + term
-                    rows = pl.ds((x + 2) * pitch + y + 2, 3, stride=pitch)
-                    grid[group, rows, :] += c_in[k, pl.ds(C_OFFSET[level, term, group], 3), :]
-        if level:
-            near_depth(level, grid, mixes[level], 0, size_x + 5)
-            near_rest(level, mixes[level], weights, fields[level], 0, size_x + 1)
-        else:
-            near_depth(0, grid, mixed0, 0, 3)
-            near_depth(0, grid, mixed0, 18, 3)
-            near_rest(0, mixed0, weights, out, 0, 3)
-            near_rest(0, mixed0, weights, out, 14, 17)
+        add_corners(level)
+        near_depth(level, grid, mixes[level], 0, size_x + 5)
+        near_rest(level, mixes[level], weights, fields[level], 0, size_x + 1)
 
     for copy in copies_b:
         copy.wait_recv()
@@ -589,21 +843,25 @@
     low = jnp.sum(kernel_hat * hat, axis=0, keepdims=True)
     high = jnp.sum(kernel_next * hat, axis=0, keepdims=True)
     pair = jnp.concatenate([low, high, jnp.zeros((6, 512), F32)], axis=0)
+    for load in loads[2:4]:
+        load.wait()
     top = dot3(pair, back_high[...], back_low[...])
-    rows_of = [[top[side : side + 1, b * 128 : b * 128 + 128] for b in range(3)] for side in range(2)]
+    ends = [[top[side : side + 1, b * 128 : b * 128 + 128] for b in range(3)] for side in range(2)]
     for plane in range(3):
         line_of = (
-            rows_of[0]
+            ends[0]
             if plane == 0
-            else rows_of[1]
+            else ends[1]
             if plane == 2
-            else [0.5 * (rows_of[0][b] + rows_of[1][b]) for b in range(3)]
+            else [0.5 * (ends[0][b] + ends[1][b]) for b in range(3)]
         )
         for y in range(5):
             value = line_of[y // 2] if y % 2 == 0 else 0.5 * (line_of[y // 2] + line_of[y // 2 + 1])
             field3[0, pl.ds(plane * 16 + y, 1), :] += value
-    for level in (2, 1, 0):
+    for level in (2, 1):
         double(level, fields[level + 1], fields[level])
+    for copy in copies_p:
+        copy.wait_recv()
     for copy in sends:
         copy.wait_send()
 
@@ -632,36 +890,65 @@
     return pair(forward) + pair(back)
 
 
+def near_tables():
+    pitch = PITCH[0]
+    tables = np.zeros((TERMS, 3, 2, pitch, 6, pitch))
+    for term, width in enumerate(WIDTHS):
+        for apart in range(3):
+            for a in range(-2, 3):
+                for b in range(-2, 3):
+                    value = math.exp(-(apart * apart + a * a + b * b) / (width * width))
+                    for plane in range(2):
+                        for y in range(COUNT_Y[0] + 1):
+                            tables[term, apart, plane, y, plane + 2 + a, y + 2 + b] = value
+    return tables.reshape(TERMS, 6 * pitch, 6 * pitch).astype(np.float32)
+
+
 def local(cells, offsets, charges, kernel_weights, screening):
-    charges_row = charges.reshape(1, PART)
+    def in_hbm(*arrays):
+        return [pltpu.with_memory_space_constraint(array, pltpu.HBM) for array in arrays]
+
+    held = in_hbm(cells, offsets, charges.reshape(1, PART))
     vmem = pl.BlockSpec(memory_space=pltpu.VMEM)
     smem = pl.BlockSpec(memory_space=pltpu.SMEM)
+    hbm = pl.BlockSpec(memory_space=pltpu.HBM)
     limit = 48 * 1024 * 1024
     grid_shape = (4, 17 * PITCH[0], 128)
+    particles = [
+        pltpu.VMEM((3, PART), jnp.int32),
+        pltpu.VMEM((3, PART), F32),
+        pltpu.VMEM((1, PART), F32),
+    ]
+    spans = [pltpu.SMEM((2 * PART // CHUNK,), jnp.int32), pltpu.SemaphoreType.DMA((3,))]
     deposited = pl.pallas_call(
         deposit_kernel,
         out_shape=jax.ShapeDtypeStruct(grid_shape, F32),
-        in_specs=[smem, vmem, vmem, vmem],
+        in_specs=[hbm, hbm, hbm],
         out_specs=vmem,
+        scratch_shapes=particles + spans,
         compiler_params=pltpu.CompilerParams(vmem_limit_bytes=limit),
         name="deposit",
-    )(cells, cells, offsets, charges_row)
+    )(*held)
 
     def rimmed(level):
         return (GROUPS[level], (COUNT_X[level] + 5) * PITCH[level] + 8, 128)
 
-    scratch = [pltpu.VMEM(rimmed(level), F32) for level in range(4)]
+    scratch = [pltpu.VMEM((512, 512), BF16)] * 2 + [pltpu.VMEM((512, 384), BF16)] * 2
+    scratch += [pltpu.VMEM((TERMS, 6 * PITCH[0], 6 * PITCH[0]), F32)]
+    scratch += [pltpu.VMEM((14 * PITCH[0], 512), BF16)] * 2
+    scratch += [pltpu.SemaphoreType.DMA((5,))]
+    scratch += [pltpu.VMEM(rimmed(level), F32) for level in (1, 2, 3)]
     scratch += [
         pltpu.VMEM((GROUPS[level], (COUNT_X[level] + 1) * PITCH[level], 128), F32) for level in (1, 2)
     ]
     scratch += [pltpu.VMEM((24, 128), F32)]
     scratch += [
         pltpu.VMEM((GROUPS[level], (COUNT_X[level] + 1) * PITCH[level], 128), F32)
-        for level in (1, 2, 3)
-    ]
-    scratch += [pltpu.VMEM((TERMS,) + rimmed(level), F32) for level in range(4)]
+        for level in (2, 3)
+    ]
+    scratch += [pltpu.VMEM((TERMS,) + rimmed(level), F32) for level in (1, 2, 3)]
     scratch += [pltpu.VMEM((2, 56, 128), F32), pltpu.VMEM((1, 40, 128), F32), pltpu.VMEM((1, 40, 128), F32)]
-    scratch += [pltpu.VMEM((2, GROUPS[level], 3 * PITCH[level], 128), F32) for level in range(3)]
+    scratch += [pltpu.VMEM((2, GROUPS[level], 3 * PITCH[level], 128), F32) for level in (1, 2)]
     scratch += [pltpu.VMEM((2, Y_ROWS, 128), F32)] * 2
     scratch += [pltpu.VMEM((4, C_ROWS, 128), F32)] * 2
     scratch += [
@@ -670,30 +957,47 @@
         pltpu.VMEM((4, 8, 128), F32),
         pltpu.VMEM(((N_GX + 1) * 8, 128), F32),
     ]
-    for count in (6, 2, 4, len(FAR3), N_GY, N_GX):
+    for count in (6, 4, 2, 4, len(FAR3), N_GY, N_GX):
         scratch += [pltpu.SemaphoreType.DMA((count,))] * 2
-    field = pl.pallas_call(
+    given = pl.pallas_call(
         field_kernel,
-        out_shape=jax.ShapeDtypeStruct(grid_shape, F32),
-        in_specs=[smem, smem] + [vmem] * 5,
-        out_specs=vmem,
+        out_shape=[
+            jax.ShapeDtypeStruct(grid_shape, F32),
+            jax.ShapeDtypeStruct((GROUPS[1], (COUNT_X[1] + 1) * PITCH[1], 128), F32),
+            jax.ShapeDtypeStruct(rimmed(0), F32),
+            jax.ShapeDtypeStruct((6 * PITCH[0], 6 * PITCH[0]), BF16),
+            jax.ShapeDtypeStruct((6 * PITCH[0], 6 * PITCH[0]), BF16),
+            jax.ShapeDtypeStruct((2, 3, PART), jnp.int32),
+            jax.ShapeDtypeStruct((2, 3, PART), F32),
+            jax.ShapeDtypeStruct((2, 1, PART), F32),
+        ],
+        in_specs=[smem, smem, vmem] + [hbm] * 8,
+        out_specs=[vmem] * 8,
         scratch_shapes=scratch,
         compiler_params=pltpu.CompilerParams(
             vmem_limit_bytes=limit, collective_id=0, has_side_effects=True
         ),
         name="field",
-    )(kernel_weights, screening, deposited, *[jnp.asarray(t) for t in transforms()])
+    )(kernel_weights, screening, deposited, *held, *in_hbm(*[jnp.asarray(t) for t in (*transforms(), near_tables())]))
     potential, forces = pl.pallas_call(
         sample_kernel,
         out_shape=[
             jax.ShapeDtypeStruct((1, PART), F32),
             jax.ShapeDtypeStruct((3, PART), F32),
         ],
-        in_specs=[smem] + [vmem] * 4,
+        in_specs=[hbm, hbm, hbm] + [vmem] * 8,
         out_specs=[vmem, vmem],
+        scratch_shapes=particles
+        + [
+            pltpu.VMEM(grid_shape, F32),
+            pltpu.VMEM((2, 4, 8 * PITCH[0], 128), F32),
+            pltpu.VMEM((2, 8 * PITCH[0], 512), BF16),
+            pltpu.VMEM((2, 8 * PITCH[0], 512), BF16),
+        ]
+        + [pltpu.VMEM((18 * PITCH[0], 640), BF16)] * 2 + spans,
         compiler_params=pltpu.CompilerParams(vmem_limit_bytes=limit),
         name="sample",
-    )(cells, cells, offsets, charges_row, field)
+    )(*held, *given)
     return (potential.reshape(PART), forces)
 
 

time: 57.8 us -> 36.2 us (0.63); the launches traced: 56.8 us -> 36.1 us
  Pallas kernels: 52.1 us -> 34.7 us
  local copies, waits for them, and re-layouts: 3.22 us -> 0.01 us
    pallas_call x1, Pallas kernels: 11 us -> 3.16 us  [local(): pl.pallas_call(deposit_kernel, out_shape=jax.ShapeDtypeStruct(grid_shape,...]
    pallas_call x1, Pallas kernels: 30.1 us -> 25.3 us  [local(): pl.pallas_call(field_kernel, out_shape=[jax.ShapeDtypeStruct(grid_shape,...]
    pallas_call x1, Pallas kernels: 10.9 us -> 6.26 us  [local(): pl.pallas_call(sample_kernel, out_shape=[jax.ShapeDtypeStruct((1, PART),...]
    unnamed x18 -> x2, local copies, waits for them, and re-layouts: 3.22 us -> 0.01 us
where the time goes in v1:
time: 36.2 us; the launch traced here: 36.1 us
  Pallas kernels  34.7 us (96%)
  between operations  1.32 us (4%)
    pallas_call x1, Pallas kernels, local(): pl.pallas_call(field_kernel, out_shape=[jax.ShapeDtypeStruct(grid_shape,...  25.3 us
    pallas_call x1, Pallas kernels, local(): pl.pallas_call(sample_kernel, out_shape=[jax.ShapeDtypeStruct((1, PART),...  6.26 us
    pallas_call x1, Pallas kernels, local(): pl.pallas_call(deposit_kernel, out_shape=jax.ShapeDtypeStruct(grid_shape,...  3.16 us

profile of v1, /device:TPU:2, one launch (start us, length us, event | category | flops | bytes accessed | tf_op | source)
XLA Modules:
  0.0 36.1 jit_solution(9136276797550891396)
XLA Ops:
  0.6 0.0 copy-start
  1.3 3.2 %deposit.1.own0 = f32[4,680,128]{2,1,0:T(8,128)S(1)} custom-call(s32[3,2048]{1,0:T(4,128)} %cells_h.5, f32[3,2048]{1,0:T(4,128)} %offsets_h.5, f32[1,2048]{1,0:T(1,128)} %bitcast.2), custom_call_target="tpu_custom_call" | custom-call | tf_op jit(solution)/shard_map/deposit/pallas_call | solution.py:923
  4.5 0.0 copy-done
  4.5 25.3 %field.1 = (f32[4,680,128]{2,1,0:T(8,128)S(1)}, f32[2,216,128]{2,1,0:T(8,128)S(1)}, f32[4,848,128]{2,1,0:T(8,128)S(1)}, bf16[240,240]{1,0:T(8,128)(2,1)S(1)}, bf...) custom-call(f32[4,3]{1,0:T(4,128)S(1)} %copy-done, ...), custom_call_target="tpu_custom_call" | custom-call | tf_op jit(solution)/shard_map/field/pallas_call | solution.py:962
  29.8 6.3 %sample.1 = (f32[1,2048]{1,0:T(1,128)}, f32[3,2048]{1,0:T(4,128)}) custom-call(s32[3,2048]{1,0:T(4,128)} %cells_h.5, f32[3,2048]{1,0:T(4,128)} %offsets_h.5, f32[1,2048]{1,0:T(1,128)} %bitcast.4, f32[4,680,128]{2,1,0:T(8,128)S(1)} %get-tuple-element.12.near, f32[2,216,128]{2,1,0:T(8,128)S(1)} %get-tuple-element.13.coarse, ...), custom_call_target="tpu_custom_call" | custom-call | tf_op jit(solution)/shard_map/sample/pallas_call | solution.py:982
Async XLA Ops:
  0.6 3.8 %copy-start = (f32[4,3]{1,0:T(4,128)S(1)}, f32[4,3]{1,0:T(4,128)}, u32[]{:S(2)}) copy-start(f32[4,3]{1,0:T(4,128)} %weights.1) | copy-start | bytes 148

commit v2 on v1

--- a/solution.py
+++ b/solution.py
@@ -321,13 +321,42 @@
         last = now
 
 
+def halo_chunk(edge, beside_cells, beside_offsets, beside_charges, side, chunk):
+    part = pl.ds(pl.multiple_of(chunk * CHUNK, CHUNK), CHUNK)
+    base = CX - 2 if side == 0 else 0
+    values = spread(
+        rows_of(beside_cells, part, side),
+        rows_of(beside_offsets, part, side),
+        beside_charges[side, 0:1, part],
+        base,
+        base,
+        HALO_PLANES,
+    )
+    for group in range(4):
+        edge[side, group, pl.ds(4 * side * PITCH[0], HALO_PLANES * PITCH[0]), :] += values[group]
+
+
+def near_edge(side, edge, edge_high, edge_low, table_high, table_low, store):
+    pitch = PITCH[0]
+    for group in range(4):
+        high, low = split(edge[side, group])
+        edge_high[side, :, group * 128 : group * 128 + 128] = high
+        edge_low[side, :, group * 128 : group * 128 + 128] = low
+    for window in range(2):
+        values = near_pair(table_high, table_low, edge_high.at[side], edge_low.at[side], window * 2 * pitch)
+        planes = 1 if side and window else 2
+        store(
+            pl.ds((14 * side + 2 * window) * pitch, planes * pitch),
+            [value[: planes * pitch] for value in values],
+        )
+
+
 def sample_kernel(
     cells_h,
     offsets_h,
     charges_h,
     near,
     coarse,
-    grid,
     table_high,
     table_low,
     beside_cells,
@@ -350,60 +379,35 @@
     copies = load_particles((cells_h, offsets_h, charges_h), (cells_v, offsets_v, charges_v), sems)
     pitch, width = PITCH[0], SAMPLE_PLANES
 
-    for side in range(2):
-        count = (8 - side) * pitch
-        edge[side, :, pl.ds(0, count), :] = grid[:, pl.ds(side * 14 * pitch, count), :]
-        if side:
-            edge[side, :, pl.ds(count, pitch), :] = jnp.zeros((4, pitch, 128), F32)
-        target = 4 * side * pitch
-        base = CX - 2 if side == 0 else 0
-
-        def visit(chunk):
-            part = pl.ds(pl.multiple_of(chunk * CHUNK, CHUNK), CHUNK)
-            values = spread(
-                rows_of(beside_cells, part, side),
-                rows_of(beside_offsets, part, side),
-                beside_charges[side, 0:1, part],
-                base,
-                base,
-                HALO_PLANES,
-            )
-            for group in range(4):
-                edge[side, group, pl.ds(target, HALO_PLANES * pitch), :] += values[group]
-
-        chunks = PART // CHUNK
-        spans = plane_spans(beside_cells, side)
-        if side == 0:
-            own_chunks = range(chunks - HALO_CHUNKS, chunks)
-            passed = sum((last < CX - 3).astype(jnp.int32) for _, last in spans)
-            low, high = passed, chunks - HALO_CHUNKS
-        else:
-            own_chunks = range(HALO_CHUNKS)
-            reached = sum((first < 3).astype(jnp.int32) for first, _ in spans)
-            low, high = HALO_CHUNKS, reached
-        for chunk in own_chunks:
-            visit(chunk)
-
-        def more(chunk, carry):
-            visit(chunk)
-            return carry
-
-        lax.fori_loop(low, high, more, 0)
-        for group in range(4):
-            high, low = split(edge[side, group])
-            edge_high[side, :, group * 128 : group * 128 + 128] = high
-            edge_low[side, :, group * 128 : group * 128 + 128] = low
-        for window in range(2):
-            values = near_pair(
-                table_high, table_low, edge_high.at[side], edge_low.at[side], window * 2 * pitch
-            )
-            planes = 1 if side and window else 2
-            for group in range(4):
-                field[group, pl.ds((14 * side + 2 * window) * pitch, planes * pitch), :] = values[group][
-                    : planes * pitch
-                ]
-    field[:, pl.ds(4 * pitch, 10 * pitch), :] = near[:, pl.ds(4 * pitch, 10 * pitch), :]
+    field[...] = near[...]
     double(0, coarse, field)
+
+    chunks = PART // CHUNK
+
+    def planes_of(side, chunk):
+        part = slice(chunk * CHUNK, (chunk + 1) * CHUNK)
+        return (beside_cells[side, 0:1, part] & (CX - 1)).astype(F32)
+
+    more_low = jnp.max(planes_of(0, chunks - HALO_CHUNKS - 1)) >= CX - HALO_PLANES
+    more_high = jnp.min(planes_of(1, HALO_CHUNKS)) < HALO_PLANES
+
+    @pl.when(more_low | more_high)
+    def _():
+        for side in range(2):
+            edge[side] = jnp.zeros_like(edge[side])
+            first = 0 if side == 0 else HALO_CHUNKS
+
+            def one_chunk(chunk, carry):
+                halo_chunk(edge, beside_cells, beside_offsets, beside_charges, side, chunk)
+                return carry
+
+            lax.fori_loop(first, first + chunks - HALO_CHUNKS, one_chunk, 0)
+
+            def store(rows, values):
+                for group in range(4):
+                    field[group, rows, :] += values[group]
+
+            near_edge(side, edge, edge_high, edge_low, table_high, table_low, store)
 
     for group in range(5):
         values = field[group] if group < 4 else turn(field[0], -1)
@@ -493,12 +497,15 @@
     tables_h,
     out,
     field1,
-    grid0,
     table_high,
     table_low,
     beside_cells,
     beside_offsets,
     beside_charges,
+    grid0,
+    edge,
+    edge_high,
+    edge_low,
     forward_high,
     forward_low,
     back_high,
@@ -614,6 +621,47 @@
         )
         stage1[0, pl.ds(4 * side, 4), :] = result[0:4]
 
+    for level in range(3):
+        count = COUNT_X[level] + 1
+        for term in range(3):
+            for group in range(GROUPS[level]):
+                for side in range(2):
+                    y = term if side == 0 else COUNT_Y[level] - 2 + term
+                    y_out[side, pl.ds(Y_OFFSET[level, term, group], count), :] = own[level][
+                        group, pl.ds(2 + y, count, stride=PITCH[level]), :
+                    ]
+    for (level, term, group), place in C_OFFSET.items():
+        for side_x in range(2):
+            start = 0 if side_x == 0 else COUNT_X[level] - 2
+            for side_y in range(2):
+                c_out[2 * side_x + side_y, pl.ds(place, 3), :] = y_out[
+                    side_y, pl.ds(Y_OFFSET[level, term, group] + start, 3), :
+                ]
+    line = lax.broadcasted_iota(jnp.int32, (N_GX, 512), 0)
+    column = lax.broadcasted_iota(jnp.int32, (N_GX, 512), 1)
+    top_y = ((column >> 5) & 3) * 4 + (column >> 7)
+    top_z = column & 31
+    far_x = jnp.minimum(line, N_GX - line)
+    far_y = jnp.minimum(top_y, 16 - top_y)
+    far_z = jnp.minimum(top_z, 32 - top_z)
+    squared = (far_x * far_x + far_y * far_y + far_z * far_z).astype(F32)
+    kernel = jnp.exp(-screening[0, 0] * jnp.sqrt(squared)) / jnp.sqrt(1.0 + squared)
+    for load in loads[:2]:
+        load.wait()
+    kernel_hat = dot3(kernel, forward_high[...], forward_low[...])
+    loads[4].wait()
+    table = weights[0, 0] * tables[0] + weights[0, 1] * tables[1] + weights[0, 2] * tables[2]
+    high, low = split(table)
+    table_high[...] = high
+    table_low[...] = low
+    kernel_next = pltpu.roll(kernel_hat, N_GX - 1, 0)
+    for start, count in ((0, 2), (19, 2)):
+        grid0[:, pl.ds(start * PITCH[0], count * PITCH[0]), :] = jnp.zeros((4, count * PITCH[0], 128), F32)
+    grid0[:, pl.ds(2 * PITCH[0], 17 * PITCH[0]), :] = own0[...]
+    for level in range(1, 4):
+        near_tail(level, mixes[level])
+    edge[...] = jnp.zeros_like(edge)
+
     pl.semaphore_wait(barrier, len(peers))
 
     sends = []
@@ -654,30 +702,6 @@
         for k, (source, landing) in enumerate(particles)
         for side in range(2)
     ]
-    for level in range(3):
-        count = COUNT_X[level] + 1
-        for term in range(3):
-            for group in range(GROUPS[level]):
-                for side in range(2):
-                    y = term if side == 0 else COUNT_Y[level] - 2 + term
-                    y_out[side, pl.ds(Y_OFFSET[level, term, group], count), :] = own[level][
-                        group, pl.ds(2 + y, count, stride=PITCH[level]), :
-                    ]
-    copies_y = [
-        send(y_out.at[side], y_in.at[1 - side], y_send.at[side], y_recv.at[side], 0, 2 * side - 1)
-        for side in range(2)
-    ]
-    copies_3 = [
-        send(own3.at[far_rows(dx)], in3.at[k, far_rows(dx)], send3.at[k], recv3.at[k], -dx, -dy)
-        for k, (dx, dy) in enumerate(FAR3)
-    ]
-    for (level, term, group), place in C_OFFSET.items():
-        for side_x in range(2):
-            start = 0 if side_x == 0 else COUNT_X[level] - 2
-            for side_y in range(2):
-                c_out[2 * side_x + side_y, pl.ds(place, 3), :] = y_out[
-                    side_y, pl.ds(Y_OFFSET[level, term, group] + start, 3), :
-                ]
     copies_c = [
         send(
             c_out.at[k],
@@ -689,8 +713,12 @@
         )
         for k in range(4)
     ]
+    copies_y = [
+        send(y_out.at[side], y_in.at[1 - side], y_send.at[side], y_recv.at[side], 0, 2 * side - 1)
+        for side in range(2)
+    ]
     copies_x = []
-    for level, landing in ((2, x2), (1, x1)):
+    for level, landing in ((1, x1), (2, x2)):
         pitch = PITCH[level]
         for side in range(2):
             start = 0 if side == 0 else (COUNT_X[level] - 2) * pitch
@@ -705,25 +733,10 @@
                 )
             )
 
-    line = lax.broadcasted_iota(jnp.int32, (N_GX, 512), 0)
-    column = lax.broadcasted_iota(jnp.int32, (N_GX, 512), 1)
-    top_y = ((column >> 5) & 3) * 4 + (column >> 7)
-    top_z = column & 31
-    far_x = jnp.minimum(line, N_GX - line)
-    far_y = jnp.minimum(top_y, 16 - top_y)
-    far_z = jnp.minimum(top_z, 32 - top_z)
-    squared = (far_x * far_x + far_y * far_y + far_z * far_z).astype(F32)
-    kernel = jnp.exp(-screening[0] * jnp.sqrt(squared)) / jnp.sqrt(1.0 + squared)
-    for load in loads[:2]:
-        load.wait()
-    kernel_hat = dot3(kernel, forward_high[...], forward_low[...])
-    loads[4].wait()
-    table = weights[0, 0] * tables[0] + weights[0, 1] * tables[1] + weights[0, 2] * tables[2]
-    high, low = split(table)
-    table_high[...] = high
-    table_low[...] = low
-    kernel_next = pltpu.roll(kernel_hat, N_GX - 1, 0)
-
+    copies_3 = [
+        send(own3.at[far_rows(dx)], in3.at[k, far_rows(dx)], send3.at[k], recv3.at[k], -dx, -dy)
+        for k, (dx, dy) in enumerate(FAR3)
+    ]
     for copy in copies_a:
         copy.wait_recv()
     for side in range(2):
@@ -759,11 +772,6 @@
         for d in range(1, N_GX)
     ]
 
-    for start, count in ((0, 2), (19, 2)):
-        grid0[:, pl.ds(start * PITCH[0], count * PITCH[0]), :] = jnp.zeros((4, count * PITCH[0], 128), F32)
-    grid0[:, pl.ds(2 * PITCH[0], 17 * PITCH[0]), :] = own0[...]
-    for level in range(1, 4):
-        near_tail(level, mixes[level])
     for copy in copies_y:
         copy.wait_recv()
     for level in range(3):
@@ -785,6 +793,50 @@
         for group in range(4):
             out[group, pl.ds((4 + 2 * window) * PITCH[0], 2 * PITCH[0]), :] = values[group]
 
+    for copy in copies_p:
+        copy.wait_recv()
+    chunks = PART // CHUNK
+    for side in range(2):
+        for k in range(HALO_CHUNKS):
+            chunk = chunks - 1 - k if side == 0 else k
+            halo_chunk(edge, beside_cells, beside_offsets, beside_charges, side, chunk)
+
+    for copy in copies_c:
+        copy.wait_recv()
+
+    def add_corners(level):
+        for term in range(3):
+            for group in range(GROUPS[level]):
+                for k in range(4):
+                    x = -2 if k // 2 == 0 else COUNT_X[level]
+                    y = term - 2 if k % 2 == 0 else COUNT_Y[level] + term
+                    rows = pl.ds((x + 2) * PITCH[level] + y + 2, 3, stride=PITCH[level])
+                    grids[level][group, rows, :] += c_in[k, pl.ds(C_OFFSET[level, term, group], 3), :]
+
+    add_corners(0)
+    pitch = PITCH[0]
+    for side in range(2):
+        count = (8 - side) * pitch
+        edge[side, :, pl.ds(0, count), :] += grid0[:, pl.ds(side * 14 * pitch, count), :]
+
+        def store(rows, values):
+            for group in range(4):
+                out[group, rows, :] = values[group]
+
+        near_edge(side, edge, edge_high, edge_low, table_high, table_low, store)
+    for number, (level, landing) in enumerate(((1, x1), (2, x2))):
+        pitch, size_x, grid = PITCH[level], COUNT_X[level], grids[level]
+        for copy in copies_x[2 * number : 2 * number + 2]:
+            copy.wait_recv()
+        grid[:, pl.ds(0, 2 * pitch), :] = landing[0, :, pl.ds(0, 2 * pitch), :]
+        grid[:, pl.ds(2 * pitch, pitch), :] += landing[0, :, pl.ds(2 * pitch, pitch), :]
+        start = (size_x + 2) * pitch
+        grid[:, pl.ds(start, pitch), :] += landing[1, :, pl.ds(0, pitch), :]
+        grid[:, pl.ds(start + pitch, 2 * pitch), :] = landing[1, :, pl.ds(pitch, 2 * pitch), :]
+        add_corners(level)
+        near_depth(level, grid, mixes[level], 0, size_x + 5)
+        near_rest(level, mixes[level], weights, fields[level], 0, size_x + 1)
+
     for copy in copies_3:
         copy.wait_recv()
     for k, (dx, dy) in enumerate(FAR3):
@@ -804,31 +856,8 @@
         )
         field3[0, pl.ds(plane * 16 + 8, 8), :] = jnp.zeros((8, 128), F32)
 
-    for copy in copies_c:
-        copy.wait_recv()
-
-    def add_corners(level):
-        for term in range(3):
-            for group in range(GROUPS[level]):
-                for k in range(4):
-                    x = -2 if k // 2 == 0 else COUNT_X[level]
-                    y = term - 2 if k % 2 == 0 else COUNT_Y[level] + term
-                    rows = pl.ds((x + 2) * PITCH[level] + y + 2, 3, stride=PITCH[level])
-                    grids[level][group, rows, :] += c_in[k, pl.ds(C_OFFSET[level, term, group], 3), :]
-
-    add_corners(0)
-    for number, (level, landing) in enumerate(((2, x2), (1, x1))):
-        pitch, size_x, grid = PITCH[level], COUNT_X[level], grids[level]
-        for copy in copies_x[2 * number : 2 * number + 2]:
-            copy.wait_recv()
-        grid[:, pl.ds(0, 2 * pitch), :] = landing[0, :, pl.ds(0, 2 * pitch), :]
-        grid[:, pl.ds(2 * pitch, pitch), :] += landing[0, :, pl.ds(2 * pitch, pitch), :]
-        start = (size_x + 2) * pitch
-        grid[:, pl.ds(start, pitch), :] += landing[1, :, pl.ds(0, pitch), :]
-        grid[:, pl.ds(start + pitch, 2 * pitch), :] = landing[1, :, pl.ds(pitch, 2 * pitch), :]
-        add_corners(level)
-        near_depth(level, grid, mixes[level], 0, size_x + 5)
-        near_rest(level, mixes[level], weights, fields[level], 0, size_x + 1)
+    for level in (2, 1):
+        double(level, fields[level + 1], fields[level])
 
     for copy in copies_b:
         copy.wait_recv()
@@ -846,22 +875,21 @@
     for load in loads[2:4]:
         load.wait()
     top = dot3(pair, back_high[...], back_low[...])
-    ends = [[top[side : side + 1, b * 128 : b * 128 + 128] for b in range(3)] for side in range(2)]
-    for plane in range(3):
-        line_of = (
-            ends[0]
-            if plane == 0
-            else ends[1]
-            if plane == 2
-            else [0.5 * (ends[0][b] + ends[1][b]) for b in range(3)]
-        )
-        for y in range(5):
-            value = line_of[y // 2] if y % 2 == 0 else 0.5 * (line_of[y // 2] + line_of[y // 2 + 1])
-            field3[0, pl.ds(plane * 16 + y, 1), :] += value
-    for level in (2, 1):
-        double(level, fields[level + 1], fields[level])
-    for copy in copies_p:
-        copy.wait_recv()
+    row = lax.broadcasted_iota(jnp.int32, (PITCH[1], 128), 0)
+    hats = [jnp.maximum(8 - jnp.abs(row - 8 * b), 0).astype(F32) * 0.125 for b in range(3)]
+    for group in range(2):
+        levels = [top[:, b * 128 : b * 128 + 128] for b in range(3)]
+        if group:
+            levels = [0.5 * (v + turn(v, -1)) for v in levels]
+        low, high = [
+            hats[0] * levels[0][side : side + 1]
+            + hats[1] * levels[1][side : side + 1]
+            + hats[2] * levels[2][side : side + 1]
+            for side in range(2)
+        ]
+        step = 0.125 * (high - low)
+        for plane in range(COUNT_X[1] + 1):
+            field1[group, pl.ds(plane * PITCH[1], PITCH[1]), :] += low + float(plane) * step
     for copy in sends:
         copy.wait_send()
 
@@ -933,7 +961,11 @@
     def rimmed(level):
         return (GROUPS[level], (COUNT_X[level] + 5) * PITCH[level] + 8, 128)
 
-    scratch = [pltpu.VMEM((512, 512), BF16)] * 2 + [pltpu.VMEM((512, 384), BF16)] * 2
+    scratch = [pltpu.VMEM(rimmed(0), F32)]
+    edges = [pltpu.VMEM((2, 4, 8 * PITCH[0], 128), F32)]
+    edges += [pltpu.VMEM((2, 8 * PITCH[0], 512), BF16)] * 2
+    scratch += edges
+    scratch += [pltpu.VMEM((512, 512), BF16)] * 2 + [pltpu.VMEM((512, 384), BF16)] * 2
     scratch += [pltpu.VMEM((TERMS, 6 * PITCH[0], 6 * PITCH[0]), F32)]
     scratch += [pltpu.VMEM((14 * PITCH[0], 512), BF16)] * 2
     scratch += [pltpu.SemaphoreType.DMA((5,))]
@@ -964,7 +996,6 @@
         out_shape=[
             jax.ShapeDtypeStruct(grid_shape, F32),
             jax.ShapeDtypeStruct((GROUPS[1], (COUNT_X[1] + 1) * PITCH[1], 128), F32),
-            jax.ShapeDtypeStruct(rimmed(0), F32),
             jax.ShapeDtypeStruct((6 * PITCH[0], 6 * PITCH[0]), BF16),
             jax.ShapeDtypeStruct((6 * PITCH[0], 6 * PITCH[0]), BF16),
             jax.ShapeDtypeStruct((2, 3, PART), jnp.int32),
@@ -972,28 +1003,24 @@
             jax.ShapeDtypeStruct((2, 1, PART), F32),
         ],
         in_specs=[smem, smem, vmem] + [hbm] * 8,
-        out_specs=[vmem] * 8,
+        out_specs=[vmem] * 7,
         scratch_shapes=scratch,
         compiler_params=pltpu.CompilerParams(
             vmem_limit_bytes=limit, collective_id=0, has_side_effects=True
         ),
         name="field",
-    )(kernel_weights, screening, deposited, *held, *in_hbm(*[jnp.asarray(t) for t in (*transforms(), near_tables())]))
+    )(kernel_weights, screening.reshape(1, 1), deposited, *held, *in_hbm(*[jnp.asarray(t) for t in (*transforms(), near_tables())]))
     potential, forces = pl.pallas_call(
         sample_kernel,
         out_shape=[
             jax.ShapeDtypeStruct((1, PART), F32),
             jax.ShapeDtypeStruct((3, PART), F32),
         ],
-        in_specs=[hbm, hbm, hbm] + [vmem] * 8,
+        in_specs=[hbm, hbm, hbm] + [vmem] * 7,
         out_specs=[vmem, vmem],
         scratch_shapes=particles
-        + [
-            pltpu.VMEM(grid_shape, F32),
-            pltpu.VMEM((2, 4, 8 * PITCH[0], 128), F32),
-            pltpu.VMEM((2, 8 * PITCH[0], 512), BF16),
-            pltpu.VMEM((2, 8 * PITCH[0], 512), BF16),
-        ]
+        + [pltpu.VMEM(grid_shape, F32)]
+        + edges
         + [pltpu.VMEM((18 * PITCH[0], 640), BF16)] * 2 + spans,
         compiler_params=pltpu.CompilerParams(vmem_limit_bytes=limit),
         name="sample",

time: 36.2 us -> 35.1 us (0.970)
  the two profiles are of different devices: /device:TPU:2 before, /device:TPU:1 now
where the time goes in v2:
time: 35.1 us; the launch traced here: 34.8 us
  Pallas kernels  33.4 us (95%)
  between operations  1.48 us (4%)
    pallas_call x1, Pallas kernels, local(): pl.pallas_call(field_kernel, out_shape=[jax.ShapeDtypeStruct(grid_shape,...  25.9 us
    pallas_call x1, Pallas kernels, local(): pl.pallas_call(sample_kernel, out_shape=[jax.ShapeDtypeStruct((1, PART),...  4.34 us
    pallas_call x1, Pallas kernels, local(): pl.pallas_call(deposit_kernel, out_shape=jax.ShapeDtypeStruct(grid_shape,...  3.15 us

profile of v2, /device:TPU:1, one launch (start us, length us, event | category | flops | bytes accessed | tf_op | source)
XLA Modules:
  0.0 34.8 jit_solution(8242165632225831067)
XLA Ops:
  0.6 0.0 copy-start
  1.3 3.1 %deposit.1.own0 = f32[4,680,128]{2,1,0:T(8,128)S(1)} custom-call(s32[3,2048]{1,0:T(4,128)} %cells_h.5, f32[3,2048]{1,0:T(4,128)} %offsets_h.5, f32[1,2048]{1,0:T(1,128)} %bitcast.4), custom_call_target="tpu_custom_call" | custom-call | tf_op jit(solution)/shard_map/deposit/pallas_call | solution.py:951
  4.5 0.0 copy-done
  4.5 25.9 %field.1 = (f32[4,680,128]{2,1,0:T(8,128)S(1)}, f32[2,216,128]{2,1,0:T(8,128)S(1)}, bf16[240,240]{1,0:T(8,128)(2,1)S(1)}, bf16[240,240]{1,0:T(8,128)(2,1)S(1)}, ...) custom-call(f32[4,3]{1,0:T(4,128)S(1)} %copy-done, f32[1,1]{1,0:T(1,128)} %bitcast.3.screening, ...), custom_call_target="tpu_custom_call" | custom-call | tf_op jit(solution)/shard_map/field/pallas_call | solution.py:994
  30.3 4.3 %sample.1 = (f32[1,2048]{1,0:T(1,128)}, f32[3,2048]{1,0:T(4,128)}) custom-call(s32[3,2048]{1,0:T(4,128)} %cells_h.5, f32[3,2048]{1,0:T(4,128)} %offsets_h.5, f32[1,2048]{1,0:T(1,128)} %bitcast.6, f32[4,680,128]{2,1,0:T(8,128)S(1)} %get-tuple-element.11.near, f32[2,216,128]{2,1,0:T(8,128)S(1)} %get-tuple-element.12.coarse, ...), custom_call_target="tpu_custom_call" | custom-call | tf_op jit(solution)/shard_map/sample/pallas_call | solution.py:1013
Async XLA Ops:
  0.6 3.8 %copy-start = (f32[4,3]{1,0:T(4,128)S(1)}, f32[4,3]{1,0:T(4,128)}, u32[]{:S(2)}) copy-start(f32[4,3]{1,0:T(4,128)} %weights.1) | copy-start | bytes 148
